TPU v7x, 32 devices: a whole 2x2x4 slice. The times are simulated.
32 devices in a mesh: tok: 4 (over y, x), gr: 2 (over core), gc: 4 (over z).
Axes of the slice: x: 2, y: 2, z: 4, core: 2. Of those that a mesh axis runs over, the one named last changes fastest.
Arguments:
- acts: bfloat16 [512, 16384], P('tok', ('gr', 'gc')), may hold values from -24 to 24
- init_basis: float32 [16, 1024, 512], P(('gr', 'gc'), 'tok'), may hold values from -6 to 6
- kept: int32 [16, 16], replicated, may hold values from 0 to 1, as said below
- member: int32 [16], replicated, may hold values from 0 to 1, as said below
Outputs:
- bases: float32 [16, 1024, 512], P(('gr', 'gc'), 'tok')
- latent: bfloat16 [512, 1024], P(('tok', 'gr', 'gc'))
Inputs may be any that keep to these rules, and one draw needn't show every extreme that they name: kept is symmetric with ones on the diagonal. `member`: each of the 2 group numbers names exactly 8 blocks.
All inputs are finite; a program needn't handle non-finite values.
Results may differ from a plain program's by a relative error of at most 0.0095.
Values may be sent and summed in bfloat16 or wider, within the bound.
No kernel may reach another device: no remote copies, remote signals or barrier semaphores. Data moves between devices by JAX's collectives and lax.ppermute only.
A program may use at most 64 MiB of HBM per device.

v0:
```python
import math

import jax
import jax.numpy as jnp
from jax import lax
from jax.sharding import PartitionSpec as P

GBLK = 8
ITERS = 2


ridge = 2.0


def own_solve(lower_own, image):
    solved = []
    for index in range(image.shape[0]):
        solved.append(
            jax.scipy.linalg.solve_triangular(lower_own[index], image[index].T, lower=True).T
        )
    return jnp.stack(solved)


def per_device(acts, init_basis, kept, member):
    highest = lax.Precision.HIGHEST
    owned = init_basis.shape[0]
    slice_rows = init_basis.shape[1]
    rank_cols = init_basis.shape[2]
    tok_count = lax.axis_size("tok")
    block_cols = slice_rows * tok_count
    tok_rows = acts.shape[0]
    total_tokens = tok_rows * tok_count
    groups = kept.shape[0] // GBLK
    group_cols = GBLK * block_cols
    first = lax.axis_index(("gr", "gc")) * owned
    tok_pos = lax.axis_index("tok")
    links = (member[:, None] == member[None, :]).astype(jnp.int32) * kept
    own_links = lax.dynamic_slice_in_dim(links, first, owned, 0).astype(jnp.bfloat16)
    own_groups = lax.dynamic_slice_in_dim(member, first, owned, 0)
    selector = (own_groups[:, None] == jnp.arange(groups, dtype=jnp.int32)[None, :]).astype(
        jnp.float32
    )
    blocks_x = acts.reshape(tok_rows, owned, block_cols)

    def full_rows(basis_slice):
        return lax.all_gather(basis_slice.astype(jnp.bfloat16), "tok", axis=1, tiled=True)

    basis = init_basis
    basis_bf = full_rows(init_basis)
    for step in range(ITERS):
        proj = jnp.einsum(
            "tob,obr->otr", blocks_x, basis_bf, preferred_element_type=jnp.float32
        ).astype(jnp.bfloat16)
        mixed = jnp.einsum(
            "ok,ktr->otr",
            own_links,
            lax.all_gather(proj, ("gr", "gc"), axis=0, tiled=True),
            preferred_element_type=jnp.float32,
        )
        local_cover = jnp.einsum(
            "tob,otr->obr", blocks_x, mixed.astype(jnp.bfloat16), preferred_element_type=jnp.float32
        )
        summed = lax.psum_scatter(local_cover, "tok", scatter_dimension=1, tiled=True)
        own_rows = lax.dynamic_slice_in_dim(basis_bf, tok_pos * slice_rows, slice_rows, 1)
        image = summed / total_tokens + ridge * own_rows.astype(jnp.float32)
        grams = jnp.einsum("obr,obs->ors", image, image, precision=highest)
        stacked = jnp.einsum("og,ors->grs", selector, grams, precision=highest)
        gram = lax.psum(stacked, ("tok", "gr", "gc"))
        lower = jnp.linalg.cholesky(gram / group_cols)
        own_lower = jnp.einsum("og,grs->ors", selector, lower, precision=highest)
        basis = own_solve(own_lower, image)
        basis_bf = full_rows(basis)
    codes = jnp.einsum("tob,obr->otr", blocks_x, basis_bf, preferred_element_type=jnp.float32)
    placed = jnp.einsum("og,otr->tgr", selector, codes, precision=highest)
    latent = lax.psum_scatter(
        placed.reshape(
            tok_rows // lax.axis_size(("gr", "gc")) * lax.axis_size(("gr", "gc")),
            groups * rank_cols,
        ),
        ("gr", "gc"),
        scatter_dimension=0,
        tiled=True,
    )
    latent = latent * (1.0 / math.sqrt(group_cols))
    return (basis, latent.astype(jnp.bfloat16))


def solution(mesh):
    placed = (P("tok", ("gr", "gc")), P(("gr", "gc"), "tok", None), P(), P())
    return jax.shard_map(
        per_device,
        mesh=mesh,
        in_specs=placed,
        out_specs=(P(("gr", "gc"), "tok", None), P(("tok", "gr", "gc"), None)),
        check_vma=False,
    )
```

profile of v0, /device:TPU:0, one launch (start us, length us, event | category | flops | bytes accessed | tf_op | source)
XLA Modules:
  0.0 1221.1 jit_solution(16671806295809969628)
XLA Ops:
  9.4 39.0 %all-gather.6.cloned.1.call-done = bf16[2,1024,512]{2,1,0:T(8,128)(2,1)} async-done(((bf16[2,256,512]{2,1,0:T(8,128)(2,1)}), bf16[2,1024,512]{2,1,0:T(8,128)(2,1)}) %all-gather.6.cloned.1.call-update) | async-done | bytes 2097168 | tf_op jit(solution)/shard_map/all_gather | solution.py:46
  51.4 29.1 %all-gather.8.cloned.1.call-done = bf16[16,128,512]{2,1,0:T(8,128)(2,1)} async-done(((bf16[2,128,512]{2,1,0:T(8,128)(2,1)}), bf16[16,128,512]{2,1,0:T(8,128)(2,1)}) %all-gather.8.cloned.1.call-update) | async-done | bytes 2097168 | tf_op jit(solution)/shard_map/all_gather | solution.py:57
  86.2 52.3 %reduce-scatter.4.cloned.1.call-done = f32[2,256,512]{2,1,0:T(8,128)} async-done(((f32[2,1024,512]{2,1,0:T(8,128)}), f32[2,256,512]{2,1,0:T(8,128)}) %reduce-scatter.4.cloned.1.call-update) | async-done | bytes 1048592 | tf_op jit(solution)/shard_map/reduce_scatter | solution.py:63
  151.6 131.8 %all-reduce.4.cloned.1.call-done = f32[2,512,512]{1,2,0:T(8,128)} async-done(((f32[2,512,512]{1,2,0:T(8,128)}), f32[2,512,512]{1,2,0:T(8,128)}) %all-reduce.4.cloned.1.call-update) | async-done | bytes 2097168 | tf_op jit(solution)/shard_map/psum | solution.py:68
  293.2 23.5 %custom-call.37 = f32[2,128,128]{2,1,0:T(8,128)S(1)} custom-call(f32[2,128,128]{2,1,0:T(8,128)S(1)} %cholesky.430), custom_call_target="Cholesky" | custom-call | tf_op jit(solution)/shard_map/jit(cholesky)/cholesky | solution.py:69
  340.4 23.5 %custom-call.39 = f32[2,128,128]{2,1,0:T(8,128)S(1)} custom-call(f32[2,128,128]{2,1,0:T(8,128)S(1)} %cholesky.434), custom_call_target="Cholesky" | custom-call | tf_op jit(solution)/shard_map/jit(cholesky)/cholesky | solution.py:69
  387.6 24.3 %custom-call.41 = f32[2,128,128]{2,1,0:T(8,128)S(1)} custom-call(f32[2,128,128]{2,1,0:T(8,128)} %cholesky.439), custom_call_target="Cholesky" | custom-call | tf_op jit(solution)/shard_map/jit(cholesky)/cholesky | solution.py:69
  412.5 21.1 %custom-call.42 = f32[2,1,128,128]{2,3,1,0:T(8,128)} custom-call(f32[2,1,128,128]{3,2,1,0:T(8,128)} %get-tuple-element.102), custom_call_target="InvertDiagBlocksLowerTriangular" | custom-call | tf_op jit(solution)/shard_map/jit(cholesky)/cholesky | solution.py:69
  436.3 23.6 %custom-call.43 = f32[2,128,128]{2,1,0:T(8,128)S(1)} custom-call(f32[2,128,128]{2,1,0:T(8,128)S(1)} %convolution_subtract_fusion.13), custom_call_target="Cholesky" | custom-call | tf_op jit(solution)/shard_map/jit(cholesky)/cholesky | solution.py:69
  477.8 40.5 %custom-call.44 = f32[4,128,128]{1,2,0:T(8,128)S(1)} custom-call(f32[4,128,128]{2,1,0:T(8,128)} %copy-done.14), custom_call_target="InvertDiagBlocksLowerTriangular" | custom-call | tf_op jit(solution)/shard_map/jit(_solve_triangular)/triangular_solve | solution.py:19
  536.5 39.3 %custom-call.45 = f32[4,128,128]{1,2,0:T(8,128)S(1)} custom-call(f32[4,128,128]{2,1,0:T(8,128)S(1)} %get-tuple-element.31), custom_call_target="InvertDiagBlocksLowerTriangular" | custom-call | tf_op jit(solution)/shard_map/jit(_solve_triangular)/triangular_solve | solution.py:19
  581.4 34.3 %all-gather.10.cloned.1.call-done = bf16[2,1024,512]{2,1,0:T(8,128)(2,1)} async-done(((bf16[2,256,512]{2,1,0:T(8,128)(2,1)}), bf16[2,1024,512]{2,1,0:T(8,128)(2,1)}) %all-gather.10.cloned.1.call-update) | async-done | bytes 2097168 | tf_op jit(solution)/shard_map/all_gather | solution.py:46
  619.1 29.2 %all-gather.12.cloned.1.call-done = bf16[16,128,512]{2,1,0:T(8,128)(2,1)} async-done(((bf16[2,128,512]{2,1,0:T(8,128)(2,1)}), bf16[16,128,512]{2,1,0:T(8,128)(2,1)}) %all-gather.12.cloned.1.call-update) | async-done | bytes 2097168 | tf_op jit(solution)/shard_map/all_gather | solution.py:57
  654.0 52.3 %reduce-scatter.6.cloned.1.call-done = f32[2,256,512]{2,1,0:T(8,128)} async-done(((f32[2,1024,512]{2,1,0:T(8,128)}), f32[2,256,512]{2,1,0:T(8,128)}) %reduce-scatter.6.cloned.1.call-update) | async-done | bytes 1048592 | tf_op jit(solution)/shard_map/reduce_scatter | solution.py:63
  718.2 133.0 %all-reduce.6.cloned.1.call-done = f32[2,512,512]{1,2,0:T(8,128)} async-done(((f32[2,512,512]{1,2,0:T(8,128)}), f32[2,512,512]{1,2,0:T(8,128)}) %all-reduce.6.cloned.1.call-update) | async-done | bytes 2097168 | tf_op jit(solution)/shard_map/psum | solution.py:68
  861.0 23.5 %custom-call.46 = f32[2,128,128]{2,1,0:T(8,128)S(1)} custom-call(f32[2,128,128]{2,1,0:T(8,128)S(1)} %cholesky.443), custom_call_target="Cholesky" | custom-call | tf_op jit(solution)/shard_map/jit(cholesky)/cholesky | solution.py:69
  908.2 23.5 %custom-call.48 = f32[2,128,128]{2,1,0:T(8,128)S(1)} custom-call(f32[2,128,128]{2,1,0:T(8,128)S(1)} %cholesky.447), custom_call_target="Cholesky" | custom-call | tf_op jit(solution)/shard_map/jit(cholesky)/cholesky | solution.py:69
  955.1 24.3 %custom-call.50 = f32[2,128,128]{2,1,0:T(8,128)S(1)} custom-call(f32[2,128,128]{2,1,0:T(8,128)} %cholesky.452), custom_call_target="Cholesky" | custom-call | tf_op jit(solution)/shard_map/jit(cholesky)/cholesky | solution.py:69
  980.0 21.1 %custom-call.51 = f32[2,1,128,128]{2,3,1,0:T(8,128)} custom-call(f32[2,1,128,128]{3,2,1,0:T(8,128)} %get-tuple-element.97), custom_call_target="InvertDiagBlocksLowerTriangular" | custom-call | tf_op jit(solution)/shard_map/jit(cholesky)/cholesky | solution.py:69
  1003.9 23.9 %custom-call.52 = f32[2,128,128]{2,1,0:T(8,128)S(1)} custom-call(f32[2,128,128]{2,1,0:T(8,128)S(1)} %convolution_subtract_fusion.8), custom_call_target="Cholesky" | custom-call | tf_op jit(solution)/shard_map/jit(cholesky)/cholesky | solution.py:69
  1045.9 39.5 %custom-call.53 = f32[4,128,128]{1,2,0:T(8,128)S(1)} custom-call(f32[4,128,128]{2,1,0:T(8,128)S(1)} %get-tuple-element.32), custom_call_target="InvertDiagBlocksLowerTriangular" | custom-call | tf_op jit(solution)/shard_map/jit(_solve_triangular)/triangular_solve | solution.py:19
  1096.8 39.3 %custom-call.54 = f32[4,128,128]{1,2,0:T(8,128)S(1)} custom-call(f32[4,128,128]{2,1,0:T(8,128)S(1)} %get-tuple-element.33), custom_call_target="InvertDiagBlocksLowerTriangular" | custom-call | tf_op jit(solution)/shard_map/jit(_solve_triangular)/triangular_solve | solution.py:19
  1141.1 34.2 %all-gather.14.cloned.1.call-done = bf16[2,1024,512]{1,2,0:T(8,128)(2,1)} async-done(((bf16[2,256,512]{1,2,0:T(8,128)(2,1)}), bf16[2,1024,512]{1,2,0:T(8,128)(2,1)}) %all-gather.14.cloned.1.call-update) | async-done | bytes 2097168 | tf_op jit(solution)/shard_map/all_gather | solution.py:46
  1181.3 31.3 %reduce-scatter.8.cloned.1.call-done = f32[16,1024]{1,0:T(8,128)} async-done(((f32[128,1024]{1,0:T(8,128)}), f32[16,1024]{1,0:T(8,128)}) %reduce-scatter.8.cloned.1.call-update) | async-done | bytes 65552 | tf_op jit(solution)/shard_map/reduce_scatter | solution.py:75
  (249 shorter events, 280.5 us)
Async XLA Ops:
  7.2 41.3 %copy-start.4 = (bf16[128,2048]{1,0:T(8,128)(2,1)S(1)}, bf16[128,2048]{1,0:T(8,128)(2,1)}, u32[]{:S(2)}) copy-start(bf16[128,2048]{1,0:T(8,128)(2,1)} %param.7) | copy-start | bytes 1572868
  7.2 41.3 %all-gather.6.cloned.1.call-start = ((), (), s32[]{:S(2)}) async-start(), calls=%async_computation.3 | async-start | bytes 2621440 | tf_op jit(solution)/shard_map/all_gather | solution.py:46
  9.4 42.0 %copy-start.20 = (s32[16]{0:T(128)S(1)}, s32[16]{0:T(128)}, u32[]{:S(2)}) copy-start(s32[16]{0:T(128)} %param.10) | copy-start | bytes 196
  9.4 71.1 %all-gather.8.cloned.1.call-start = ((), (), s32[]{:S(2)}) async-start(), calls=%async_computation.4 | async-start | bytes 2359296 | tf_op jit(solution)/shard_map/all_gather | solution.py:57
  51.3 87.2 %reduce-scatter.4.cloned.1.call-start = ((), (), s32[]{:S(2)}) async-start(), calls=%async_computation.5 | async-start | bytes 5242880 | tf_op jit(solution)/shard_map/reduce_scatter | solution.py:63
  51.4 90.5 %copy-start.16 = (s32[2]{0:T(128)}, s32[2]{0:T(128)S(1)}, u32[]{:S(2)}) copy-start(s32[2]{0:T(128)S(1)} %dynamic_slice.12) | copy-start | bytes 28
  86.1 197.3 %all-reduce.4.cloned.1.call-start = ((), (), s32[]{:S(2)}) async-start(), calls=%async_computation.6 | async-start | bytes 4194304 | tf_op jit(solution)/shard_map/psum | solution.py:68
  149.5 466.2 %all-gather.10.cloned.1.call-start = ((), (), s32[]{:S(2)}) async-start(), calls=%async_computation.7 | async-start | bytes 2621440 | tf_op jit(solution)/shard_map/all_gather | solution.py:46
  286.6 3.2 copy-start
  291.9 1.3 copy-start.3
  477.8 40.5 %copy-start.10 = (s32[4,2]{0,1:T(2,128)}, s32[4,2]{0,1:T(2,128)S(1)}, u32[]{:S(2)}) copy-start(s32[4,2]{0,1:T(2,128)S(1)} %get-tuple-element.331) | copy-start | bytes 100
  525.4 2.9 copy-start.11
  536.5 43.9 %copy-start.15 = (bf16[128,256]{0,1:T(8,128)(2,1)S(1)}, bf16[128,256]{0,1:T(8,128)(2,1)}, u32[]{:S(2)}) copy-start(bf16[128,256]{0,1:T(8,128)(2,1)} %copy.76) | copy-start | bytes 196612
  577.8 37.9 %copy-start.5 = (bf16[128,2048]{1,0:T(8,128)(2,1)S(1)}, bf16[128,2048]{1,0:T(8,128)(2,1)}, u32[]{:S(2)}) copy-start(bf16[128,2048]{1,0:T(8,128)(2,1)} %param.7) | copy-start | bytes 1572868
  581.3 67.0 %copy-start.18 = (s32[2]{0:T(128)S(1)}, s32[2]{0:T(128)}, u32[]{:S(2)}) copy-start(s32[2]{0:T(128)} %copy-done.16) | copy-start | bytes 28
  581.3 67.0 %copy-start.21 = (s32[16]{0:T(128)S(1)}, s32[16]{0:T(128)}, u32[]{:S(2)}) copy-start(s32[16]{0:T(128)} %param.10) | copy-start | bytes 196
  581.3 67.0 %all-gather.12.cloned.1.call-start = ((), (), s32[]{:S(2)}) async-start(), calls=%async_computation.8 | async-start | bytes 2359296 | tf_op jit(solution)/shard_map/all_gather | solution.py:57
  619.1 87.3 %reduce-scatter.6.cloned.1.call-start = ((), (), s32[]{:S(2)}) async-start(), calls=%async_computation.9 | async-start | bytes 5242880 | tf_op jit(solution)/shard_map/reduce_scatter | solution.py:63
  654.0 197.2 %all-reduce.6.cloned.1.call-start = ((), (), s32[]{:S(2)}) async-start(), calls=%async_computation.10 | async-start | bytes 4194304 | tf_op jit(solution)/shard_map/psum | solution.py:68
  717.3 458.0 %all-gather.14.cloned.1.call-start = ((), (), s32[]{:S(2)}) async-start(), calls=%async_computation.11 | async-start | bytes 2621440 | tf_op jit(solution)/shard_map/all_gather | solution.py:46
  854.3 3.2 copy-start.1
  1088.5 47.6 %copy-start.7 = (f32[512,256]{0,1:T(8,128)S(1)}, f32[512,256]{0,1:T(8,128)}, u32[]{:S(2)}) copy-start(f32[512,256]{0,1:T(8,128)} %get-tuple-element.93) | copy-start | bytes 1572868
  1138.0 37.3 %copy-start.6 = (bf16[128,2048]{1,0:T(8,128)(2,1)S(1)}, bf16[128,2048]{1,0:T(8,128)(2,1)}, u32[]{:S(2)}) copy-start(bf16[128,2048]{1,0:T(8,128)(2,1)} %param.7) | copy-start | bytes 1572868
  1141.1 71.5 %reduce-scatter.8.cloned.1.call-start = ((), (), s32[]{:S(2)}) async-start(), calls=%async_computation.12 | async-start | bytes 589824 | tf_op jit(solution)/shard_map/reduce_scatter | solution.py:75
  (9 other events, 6.6 us)
Sparse Core Ops, SparseCore 0:
  10.4 38.0 all-gather.5
  51.4 29.0 all-gather.7
  86.3 52.1 reduce-scatter.3
  149.6 133.7 all-reduce.3
  581.4 34.1 all-gather.9
  619.2 29.0 all-gather.11
  654.1 52.1 reduce-scatter.5
  717.4 133.7 all-reduce.5
  1141.2 34.0 all-gather.13
  1180.0 32.5 reduce-scatter.7
where the time goes:
time: 1230 us; the launch traced here: 1220 us
  waiting for transfers between devices  567 us (46%)
  other arithmetic  495 us (40%)
  matrix products  80.5 us (7%)
  local copies, waits for them, and re-layouts  62.5 us (5%)
  between operations  15.3 us (1%)
    another operation x32, other arithmetic, per_device(): lower = jnp.linalg.cholesky(gram / group_cols)  316 us
    psum x2, waiting for transfers between devices, per_device(): gram = lax.psum(stacked, ('tok', 'gr', 'gc'))  265 us
    another operation x10, other arithmetic, own_solve(): jax.scipy.linalg.solve_triangular(lower_own[index], image[index].T, lower...  160 us
    all_gather x3, waiting for transfers between devices, full_rows(): lax.all_gather(basis_slice.astype(jnp.bfloat16), 'tok', axis=1, tiled=True)  108 us
    reduce_scatter x2, waiting for transfers between devices, per_device(): lax.psum_scatter(local_cover, 'tok', scatter_dimension=1, tiled=True)  105 us
    all_gather x2, waiting for transfers between devices, per_device(): lax.all_gather(proj, ('gr', 'gc'), axis=0, tiled=True)  58.3 us
    another operation x59, local copies, waits for them, and re-layouts, own_solve(): jax.scipy.linalg.solve_triangular(lower_own[index], image[index].T, lower...  33.4 us
    reduce_scatter x1, waiting for transfers between devices, per_device(): lax.psum_scatter(placed.reshape(tok_rows // lax.axis_size(('gr', 'gc')) *...  31.3 us
  transfers between devices with their start and end apart: 10, of which 10 were waited for; matrix products, arithmetic and copies ran while one was open for 0% of the time, Pallas kernels for 0%

commit v1 on v0

v1 whole, which is shorter than its diff:
```python
import functools
import math

import jax
import jax.numpy as jnp
from jax import lax
from jax.experimental import pallas as pl
from jax.experimental.pallas import tpu as pltpu
from jax.sharding import PartitionSpec as P

GBLK = 8
ITERS = 2
PANEL = 128
SUB = 8

ridge = 2.0
HIGHEST = lax.Precision.HIGHEST


def eliminate(tiles, store):
    lane = lax.broadcasted_iota(jnp.int32, (1, PANEL), 1)
    lane_tile = lax.broadcasted_iota(jnp.int32, (SUB, PANEL), 1)
    tiles = list(tiles)
    for j in range(PANEL):
        s, r = divmod(j, SUB)
        row = tiles[s][r : r + 1, :]
        pivot = row[:, j : j + 1]
        unit = jnp.where(lane == j, 1.0, row)
        root = lax.rsqrt(pivot)
        root = root * (1.5 - 0.5 * pivot * root * root)
        store(j, jnp.where(lane <= j, unit, 0.0) * root)
        scaled = jnp.broadcast_to(unit * (1.0 / pivot), (SUB, PANEL))
        first = s if r < SUB - 1 else s + 1
        for q in range(first, PANEL // SUB):
            factor = tiles[q][:, j : j + 1]
            tiles[q] = jnp.where(lane_tile == j, 0.0, tiles[q]) - factor * scaled


def factor_kernel(scale, gram_ref, out_ref, inv_ref):
    groups, rank, _ = gram_ref.shape
    panels = rank // PANEL
    out_ref[...] = gram_ref[...] * scale

    def panel_step(k, carry):
        here = pl.ds(pl.multiple_of(k * PANEL, PANEL), PANEL)
        diag = [out_ref[g, here, here] for g in range(groups)]
        stores = []
        for g in range(groups):

            def store(j, row, g=g):
                inv_ref[g, j : j + 1, :] = row

            stores.append(store)
        for g in range(groups):
            eliminate([diag[g][SUB * q : SUB * (q + 1), :] for q in range(PANEL // SUB)], stores[g])
        for g in range(groups):
            inv = inv_ref[g]
            out_ref[g, here, :] = jnp.dot(
                inv, out_ref[g, here, :], preferred_element_type=jnp.float32, precision=HIGHEST
            )
            out_ref[g, here, here] = inv
        for i in range(1, panels):

            @pl.when(i > k)
            def _():
                for g in range(groups):
                    below = pl.ds(i * PANEL, PANEL)
                    out_ref[g, below, here] = jnp.zeros((PANEL, PANEL), jnp.float32)
                    upper = out_ref[g, here, :]
                    out_ref[g, below, :] -= lax.dot_general(
                        upper[:, i * PANEL : (i + 1) * PANEL],
                        upper,
                        (((0,), (0,)), ((), ())),
                        preferred_element_type=jnp.float32,
                        precision=HIGHEST,
                    )

        return carry

    lax.fori_loop(0, panels, panel_step, 0)
    for i in range(panels - 1):
        out_ref[:, i * PANEL : (i + 1) * PANEL, (i + 1) * PANEL :] = jnp.zeros(
            (groups, PANEL, rank - (i + 1) * PANEL), jnp.float32
        )


def inverse_factor(gram, scale):
    groups, rank, _ = gram.shape
    return pl.pallas_call(
        functools.partial(factor_kernel, scale),
        out_shape=jax.ShapeDtypeStruct(gram.shape, jnp.float32),
        in_specs=[pl.BlockSpec(memory_space=pltpu.VMEM)],
        out_specs=pl.BlockSpec(memory_space=pltpu.VMEM),
        scratch_shapes=[pltpu.VMEM((groups, PANEL, PANEL), jnp.float32)],
        compiler_params=pltpu.CompilerParams(vmem_limit_bytes=32 * 1024 * 1024),
        name="inverse_factor",
    )(gram)


def split(value):
    high = lax.reduce_precision(value, 8, 7)
    return high.astype(jnp.bfloat16), (value - high).astype(jnp.bfloat16)


def per_device(acts, init_basis, kept, member):
    owned = init_basis.shape[0]
    slice_rows = init_basis.shape[1]
    rank = init_basis.shape[2]
    tok_count = lax.axis_size("tok")
    block_cols = slice_rows * tok_count
    tok_rows = acts.shape[0]
    total_tokens = tok_rows * tok_count
    groups = kept.shape[0] // GBLK
    group_cols = GBLK * block_cols
    own_cols = rank // tok_count
    first = lax.axis_index(("gr", "gc")) * owned
    tok_pos = lax.axis_index("tok")
    links = (member[:, None] == member[None, :]).astype(jnp.int32) * kept
    own_links = lax.dynamic_slice_in_dim(links, first, owned, 0).astype(jnp.bfloat16)
    own_groups = lax.dynamic_slice_in_dim(member, first, owned, 0)
    selector = (own_groups[:, None] == jnp.arange(groups, dtype=jnp.int32)[None, :]).astype(
        jnp.float32
    )

    def own_slice(full):
        return lax.dynamic_slice_in_dim(full, tok_pos * own_cols, own_cols, full.ndim - 1)

    own_x = acts.reshape(tok_rows, owned, block_cols)
    full_x = lax.all_gather(acts, "tok", axis=0, tiled=True)
    full_x = full_x.reshape(total_tokens, owned, block_cols)
    basis_bf = lax.all_gather(init_basis.astype(jnp.bfloat16), "tok", axis=1, tiled=True)
    for step in range(ITERS):
        proj = jnp.einsum(
            "tob,obr->otr", full_x, own_slice(basis_bf), preferred_element_type=jnp.float32
        ).astype(jnp.bfloat16)
        mixed = jnp.einsum(
            "ok,ktr->otr",
            own_links,
            lax.all_gather(proj, ("gr", "gc"), axis=0, tiled=True),
            preferred_element_type=jnp.float32,
        ).astype(jnp.bfloat16)
        mixed = lax.all_gather(mixed, "tok", axis=2, tiled=True)
        cover = jnp.einsum("tob,otr->obr", full_x, mixed, preferred_element_type=jnp.float32)
        image = cover / total_tokens + ridge * basis_bf.astype(jnp.float32)
        grams = jnp.einsum("obr,obs->ors", own_slice(image), image, precision=HIGHEST)
        stacked = jnp.sum(selector[:, :, None, None] * grams[:, None], axis=0)
        piece = lax.psum_scatter(stacked, ("gr", "gc"), scatter_dimension=1, tiled=True)
        gram = lax.all_gather(piece, ("tok", "gr", "gc"), axis=1, tiled=True)
        inverse = inverse_factor(gram, 1.0 / group_cols)
        own_inverse = jnp.sum(selector[:, :, None, None] * inverse[None], axis=1)
        if step < ITERS - 1:
            basis_bf = jnp.einsum(
                "obr,osr->obs", image, own_inverse, precision=HIGHEST
            ).astype(jnp.bfloat16)
    rows = lax.dynamic_slice_in_dim(image, tok_pos * slice_rows, slice_rows, 1)
    basis = jnp.einsum("obr,osr->obs", rows, own_inverse, precision=HIGHEST)
    codes = sum(
        jnp.einsum("tob,obr->otr", own_x, part, preferred_element_type=jnp.float32)
        for part in split(image)
    )
    placed = jnp.sum(selector[:, None, :, None] * codes[:, :, None, :], axis=0)
    placed = lax.psum_scatter(
        placed.reshape(tok_rows, groups * rank), ("gr", "gc"), scatter_dimension=0, tiled=True
    )
    latent = jnp.concatenate(
        [
            jnp.einsum(
                "tr,sr->ts",
                placed[:, g * rank : (g + 1) * rank],
                inverse[g],
                precision=HIGHEST,
            )
            for g in range(groups)
        ],
        axis=1,
    )
    latent = latent * (1.0 / math.sqrt(group_cols))
    return (basis, latent.astype(jnp.bfloat16))


def solution(mesh):
    placed = (P("tok", ("gr", "gc")), P(("gr", "gc"), "tok", None), P(), P())
    return jax.shard_map(
        per_device,
        mesh=mesh,
        in_specs=placed,
        out_specs=(P(("gr", "gc"), "tok", None), P(("tok", "gr", "gc"), None)),
        check_vma=False,
    )
```

time: 1230 us -> 571 us (0.46)
  other arithmetic: 495 us -> 5.02 us
  waiting for transfers between devices: 567 us -> 377 us
  Pallas kernels: 0 us -> 108 us
  local copies, waits for them, and re-layouts: 62.5 us -> 13.1 us
  matrix products: 80.5 us -> 45.9 us
    another operation x48 -> x0, other arithmetic: 477 us -> none  [the longest x32 316 us: per_device(): lower = jnp.linalg.cholesky(gram / group_cols)]
    psum x2 -> x0, waiting for transfers between devices: 265 us -> none  [per_device(): gram = lax.psum(stacked, ('tok', 'gr', 'gc'))]
    all_gather x3 -> x6, waiting for transfers between devices: 108 us -> 255 us  [the longest x2 111 us: per_device(): gram = lax.all_gather(piece, ('tok', 'gr', 'gc'), axis=1, tiled=True)]
    pallas_call x0 -> x2, Pallas kernels: none -> 108 us  [inverse_factor(): pl.pallas_call(functools.partial(factor_kernel, scale), out_shape=jax.Sha...]
    reduce_scatter x3 -> x2, waiting for transfers between devices: 136 us -> 65.3 us  [per_device(): lax.psum_scatter(stacked, ('gr', 'gc'), scatter_dimension=1, tiled=True)]
    another operation x40 -> x0, matrix products: 36.3 us -> none  [the longest x28 19.1 us: own_solve(): jax.scipy.linalg.solve_triangular(lower_own[index], image[index].T, lower...]
    another operation x67 -> x0, local copies, waits for them, and re-layouts: 35.2 us -> none  [the longest x59 33.4 us: own_solve(): jax.scipy.linalg.solve_triangular(lower_own[index], image[index].T, lower...]
  transfers between devices with their start and end apart: 10 -> 11, of which waited for: 10 -> 10; matrix products, arithmetic and copies ran while one was open for 0% -> 1% of each run, Pallas kernels for 0% -> 10%
where the time goes in v1:
time: 571 us; the launch traced here: 565 us
  waiting for transfers between devices  377 us (66%)
  Pallas kernels  108 us (19%)
  matrix products  45.9 us (8%)
  between operations  14.6 us (3%)
  local copies, waits for them, and re-layouts  13.1 us (2%)
    all_gather x2, waiting for transfers between devices, per_device(): gram = lax.all_gather(piece, ('tok', 'gr', 'gc'), axis=1, tiled=True)  111 us
    pallas_call x2, Pallas kernels, inverse_factor(): pl.pallas_call(functools.partial(factor_kernel, scale), out_shape=jax.Sha...  108 us
    all_gather x2, waiting for transfers between devices, per_device(): mixed = lax.all_gather(mixed, 'tok', axis=2, tiled=True)  69.3 us
    reduce_scatter x2, waiting for transfers between devices, per_device(): lax.psum_scatter(stacked, ('gr', 'gc'), scatter_dimension=1, tiled=True)  65.3 us
    all_gather x2, waiting for transfers between devices, per_device(): lax.all_gather(proj, ('gr', 'gc'), axis=0, tiled=True)  57.1 us
    all_gather x1, waiting for transfers between devices, per_device(): lax.all_gather(init_basis.astype(jnp.bfloat16), 'tok', axis=1, tiled=True)  37.6 us
    all_gather x1, waiting for transfers between devices, per_device(): full_x = lax.all_gather(acts, 'tok', axis=0, tiled=True)  37 us
  transfers between devices with their start and end apart: 11, of which 10 were waited for; matrix products, arithmetic and copies ran while one was open for 1% of the time, Pallas kernels for 10%

profile of v1, /device:TPU:0, one launch (start us, length us, event | category | flops | bytes accessed | tf_op | source)
XLA Modules:
  0.0 564.9 jit_solution(13194053874850561451)
XLA Ops:
  7.2 2.3 copy.86
  10.7 37.6 %all-gather.9.cloned.1.call-done = bf16[2,1024,512]{1,2,0:T(8,128)(2,1)} async-done(((bf16[2,256,512]{1,2,0:T(8,128)(2,1)}), bf16[2,1024,512]{1,2,0:T(8,128)(2,1)}) %all-gather.9.cloned.1.call-update) | async-done | bytes 2097168 | tf_op jit(solution)/shard_map/all_gather | solution.py:131
  48.3 37.0 %all-gather.11.cloned.1.call-done = bf16[512,2048]{0,1:T(8,128)(2,1)} async-done(((bf16[128,2048]{0,1:T(8,128)(2,1)}), bf16[512,2048]{0,1:T(8,128)(2,1)}) %all-gather.11.cloned.1.call-update) | async-done | bytes 2097168 | tf_op jit(solution)/shard_map/all_gather | solution.py:129
  85.3 2.2 fusion.16
  88.6 29.1 %all-gather.13.cloned.1.call-done = bf16[16,512,128]{2,1,0:T(8,128)(2,1)} async-done(((bf16[2,512,128]{2,1,0:T(8,128)(2,1)}), bf16[16,512,128]{2,1,0:T(8,128)(2,1)}) %all-gather.13.cloned.1.call-update) | async-done | bytes 2097168 | tf_op jit(solution)/shard_map/all_gather | solution.py:139
  117.7 3.6 fusion.10
  121.5 34.6 %all-gather.15.cloned.1.call-done = bf16[2,512,512]{2,0,1:T(2,128)(2,1)} async-done(((bf16[2,512,128]{2,0,1:T(2,128)(2,1)}), bf16[2,512,512]{2,0,1:T(2,128)(2,1)}) %all-gather.15.cloned.1.call-update) | async-done | bytes 1048592 | tf_op jit(solution)/shard_map/all_gather | solution.py:142
  156.1 3.5 bitcast_add_fusion.1
  159.6 4.4 fusion.26
  165.0 32.6 %reduce-scatter.6.cloned.1.call-done = f32[2,16,512]{2,1,0:T(8,128)} async-done(((f32[2,128,512]{2,1,0:T(8,128)}), f32[2,16,512]{2,1,0:T(8,128)}) %reduce-scatter.6.cloned.1.call-update) | async-done | bytes 65552 | tf_op jit(solution)/shard_map/reduce_scatter | solution.py:147
  197.7 58.7 %all-gather.17.cloned.1.call-done.gram_ref = f32[2,512,512]{2,1,0:T(8,128)} async-done(((f32[2,16,512]{2,1,0:T(8,128)}), f32[2,512,512]{2,1,0:T(8,128)}) %all-gather.17.cloned.1.call-update) | async-done | bytes 2097168 | tf_op jit(solution)/shard_map/all_gather | solution.py:148
  258.1 53.9 %inverse_factor.2 = f32[2,512,512]{2,1,0:T(8,128)S(1)} custom-call(f32[2,512,512]{2,1,0:T(8,128)S(1)} %copy-done.1), custom_call_target="tpu_custom_call" | custom-call | tf_op jit(solution)/shard_map/inverse_factor/pallas_call | solution.py:89
  314.2 7.1 %convolution_convert_fusion = bf16[2,1024,512]{1,2,0:T(8,128)(2,1)S(1)} fusion(f32[2,1024,512]{1,2,0:T(8,128)S(1)} %copy-done.5, f32[2,512,512]{2,1,0:T(8,128)S(1)} %multiply_reduce_fusion.1), kind=kOutput, calls=%fused_computation.13 | convolution fusion | flops 6443499520 | bytes 8388608 | tf_op jit(solution)/shard_map/obr,osr->obs/dot_general | solution.py:152
  324.2 28.0 %all-gather.19.cloned.1.call-done = bf16[16,512,128]{2,1,0:T(8,128)(2,1)} async-done(((bf16[2,512,128]{2,1,0:T(8,128)(2,1)}), bf16[16,512,128]{2,1,0:T(8,128)(2,1)}) %all-gather.19.cloned.1.call-update) | async-done | bytes 2097168 | tf_op jit(solution)/shard_map/all_gather | solution.py:139
  352.2 3.6 fusion.13
  355.9 34.7 %all-gather.21.cloned.1.call-done = bf16[2,512,512]{2,0,1:T(2,128)(2,1)} async-done(((bf16[2,512,128]{2,0,1:T(2,128)(2,1)}), bf16[2,512,512]{2,0,1:T(2,128)(2,1)}) %all-gather.21.cloned.1.call-update) | async-done | bytes 1048592 | tf_op jit(solution)/shard_map/all_gather | solution.py:142
  390.6 3.5 bitcast_add_fusion
  394.0 4.4 fusion.22
  399.5 32.6 %reduce-scatter.8.cloned.1.call-done = f32[2,16,512]{2,1,0:T(8,128)} async-done(((f32[2,128,512]{2,1,0:T(8,128)}), f32[2,16,512]{2,1,0:T(8,128)}) %reduce-scatter.8.cloned.1.call-update) | async-done | bytes 65552 | tf_op jit(solution)/shard_map/reduce_scatter | solution.py:147
  432.5 3.1 fusion.1
  438.2 52.2 %all-gather.23.cloned.1.call-done.gram_ref = f32[2,512,512]{2,1,0:T(8,128)} async-done(((f32[2,16,512]{2,1,0:T(8,128)}), f32[2,512,512]{2,1,0:T(8,128)}) %all-gather.23.cloned.1.call-update) | async-done | bytes 2097168 | tf_op jit(solution)/shard_map/all_gather | solution.py:148
  492.1 54.0 %inverse_factor.3 = f32[2,512,512]{2,1,0:T(8,128)S(1)} custom-call(f32[2,512,512]{2,1,0:T(8,128)S(1)} %copy-done), custom_call_target="tpu_custom_call" | custom-call | tf_op jit(solution)/shard_map/inverse_factor/pallas_call | solution.py:89
  547.9 1.9 fusion.19
  552.2 5.7 %fusion.24 = f32[2,256,512]{2,1,0:T(8,128)} fusion(f32[2,512,512]{2,1,0:T(8,128)S(1)} %copy-done.8, f32[2,1024,512]{1,2,0:T(8,128)} %copy-done.2, s32[]{:T(128)S(6)} %select_n.15), kind=kOutput, calls=%fused_computation.32 | convolution fusion | flops 1610612736 | bytes 4194308 | tf_op jit(solution)/shard_map/obr,osr->obs/dot_general | solution.py:156
  (62 shorter events, 19.9 us)
Async XLA Ops:
  7.2 2.4 copy-start.9
  7.2 41.1 %all-gather.9.cloned.1.call-start = ((), (), s32[]{:S(2)}) async-start(), calls=%async_computation.3 | async-start | bytes 2621440 | tf_op jit(solution)/shard_map/all_gather | solution.py:131
  9.5 75.8 %all-gather.11.cloned.1.call-start = ((), (), s32[]{:S(2)}) async-start(), calls=%async_computation.4 | async-start | bytes 2621440 | tf_op jit(solution)/shard_map/all_gather | solution.py:129
  10.6 77.9 %copy-start.10 = (s32[16]{0:T(128)S(1)}, s32[16]{0:T(128)}, u32[]{:S(2)}) copy-start(s32[16]{0:T(128)} %param.7) | copy-start | bytes 196
  10.6 107.1 %all-gather.13.cloned.1.call-start = ((), (), s32[]{:S(2)}) async-start(), calls=%async_computation.5 | async-start | bytes 2359296 | tf_op jit(solution)/shard_map/all_gather | solution.py:139
  87.6 68.5 %copy-start.6 = (bf16[512,2048]{0,1:T(8,128)(2,1)S(1)}, bf16[512,2048]{0,1:T(8,128)(2,1)}, u32[]{:S(2)}) copy-start(bf16[512,2048]{0,1:T(8,128)(2,1)} %all-gather.11.cloned.1.call-done) | copy-start | bytes 6291460
  88.4 67.6 %all-gather.15.cloned.1.call-start = ((), (), s32[]{:S(2)}) async-start(), calls=%async_computation.6 | async-start | bytes 1310720 | tf_op jit(solution)/shard_map/all_gather | solution.py:142
  121.3 76.3 %reduce-scatter.6.cloned.1.call-start = ((), (), s32[]{:S(2)}) async-start(), calls=%async_computation.7 | async-start | bytes 589824 | tf_op jit(solution)/shard_map/reduce_scatter | solution.py:147
  159.5 4.4 copy-start.4
  165.0 91.5 %all-gather.17.cloned.1.call-start = ((), (), s32[]{:S(2)}) async-start(), calls=%async_computation.8 | async-start | bytes 2162688 | tf_op jit(solution)/shard_map/all_gather | solution.py:148
  197.7 154.5 %all-gather.19.cloned.1.call-start = ((), (), s32[]{:S(2)}) async-start(), calls=%async_computation.9 | async-start | bytes 2359296 | tf_op jit(solution)/shard_map/all_gather | solution.py:139
  256.5 1.6 copy-start.1
  312.0 2.2 copy-start.5
  321.3 1.3 copy-start.7
  323.9 66.6 %all-gather.21.cloned.1.call-start = ((), (), s32[]{:S(2)}) async-start(), calls=%async_computation.10 | async-start | bytes 1310720 | tf_op jit(solution)/shard_map/all_gather | solution.py:142
  355.8 76.3 %reduce-scatter.8.cloned.1.call-start = ((), (), s32[]{:S(2)}) async-start(), calls=%async_computation.11 | async-start | bytes 589824 | tf_op jit(solution)/shard_map/reduce_scatter | solution.py:147
  394.0 4.4 copy-start.2
  399.5 91.0 %all-gather.23.cloned.1.call-start = ((), (), s32[]{:S(2)}) async-start(), calls=%async_computation.12 | async-start | bytes 2162688 | tf_op jit(solution)/shard_map/all_gather | solution.py:148
  432.1 115.8 %reduce-scatter.10.cloned.1.call-start = ((), (), s32[]{:S(2)}) async-start(), calls=%async_computation.13 | async-start | bytes 589824
  432.4 3.5 copy-start.3
  490.5 1.6 copy-start
  547.9 4.2 copy-start.8
Sparse Core Ops, SparseCore 0:
  10.4 37.8 all-gather.8
  50.1 35.1 all-gather.10
  88.6 29.0 all-gather.12
  121.5 34.5 all-gather.14
  165.1 32.5 reduce-scatter.5
  201.0 55.3 all-gather.16
  324.1 28.0 all-gather.18
  355.9 34.5 all-gather.20
  399.6 32.5 reduce-scatter.7
  435.0 55.3 all-gather.22
  493.3 31.5 reduce-scatter.9

commit v2 on v1

v2 whole, which is shorter than its diff:
```python
import functools
import math

import jax
import jax.numpy as jnp
from jax import lax
from jax.experimental import pallas as pl
from jax.experimental.pallas import tpu as pltpu
from jax.sharding import PartitionSpec as P

GBLK = 8
ITERS = 2
PANEL = 128
SUB = 8

ridge = 2.0
HIGHEST = lax.Precision.HIGHEST


def eliminate(tiles, store):
    lane = lax.broadcasted_iota(jnp.int32, (1, PANEL), 1)
    lane_tile = lax.broadcasted_iota(jnp.int32, (SUB, PANEL), 1)
    tiles = list(tiles)
    for j in range(PANEL):
        s, r = divmod(j, SUB)
        row = tiles[s][r : r + 1, :]
        pivot = row[:, j : j + 1]
        unit = jnp.where(lane == j, 1.0, row)
        root = lax.rsqrt(pivot)
        root = root * (1.5 - 0.5 * pivot * root * root)
        store(j, jnp.where(lane <= j, unit, 0.0) * root)
        scaled = jnp.broadcast_to(unit * (1.0 / pivot), (SUB, PANEL))
        first = s if r < SUB - 1 else s + 1
        for q in range(first, PANEL // SUB):
            factor = tiles[q][:, j : j + 1]
            tiles[q] = jnp.where(lane_tile == j, 0.0, tiles[q]) - factor * scaled


def factor_kernel(scale, own_cols, rows_moved, pos_ref, pieces_ref, out_ref, work_ref, inv_ref):
    tok_count, gc_count, rows, rank = pieces_ref.shape
    panels = rank // PANEL
    tok_pos, gc_pos = pos_ref[0], pos_ref[1]
    for k in range(tok_count):
        for i in range(gc_count):
            place = ((tok_pos ^ k) * gc_count + (gc_pos ^ i)) * rows
            work_ref[pl.ds(pl.multiple_of(place, SUB), rows), :] = pieces_ref[k, i] * scale

    def panel_step(k, carry):
        here = pl.ds(pl.multiple_of(k * PANEL, PANEL), PANEL)
        diag = work_ref[here, here]

        def store(j, row):
            inv_ref[j : j + 1, :] = row

        eliminate([diag[SUB * q : SUB * (q + 1), :] for q in range(PANEL // SUB)], store)
        inv = inv_ref[...]
        work_ref[here, :] = jnp.dot(
            inv, work_ref[here, :], preferred_element_type=jnp.float32, precision=HIGHEST
        )
        work_ref[here, here] = inv
        for i in range(1, panels):

            @pl.when(i > k)
            def _():
                below = pl.ds(i * PANEL, PANEL)
                work_ref[below, here] = jnp.zeros((PANEL, PANEL), jnp.float32)
                upper = work_ref[here, :]
                work_ref[below, :] -= lax.dot_general(
                    upper[:, i * PANEL : (i + 1) * PANEL],
                    upper,
                    (((0,), (0,)), ((), ())),
                    preferred_element_type=jnp.float32,
                    precision=HIGHEST,
                )

        return carry

    lax.fori_loop(0, panels, panel_step, 0)
    for i in range(panels - 1):
        work_ref[i * PANEL : (i + 1) * PANEL, (i + 1) * PANEL :] = jnp.zeros(
            (PANEL, rank - (i + 1) * PANEL), jnp.float32
        )
    if own_cols == rank:
        out_ref[...] = work_ref[...]
    else:
        for i in range(rank // own_cols):
            row = (tok_pos ^ i) * own_cols if rows_moved else i * own_cols
            for j in range(rank // own_cols):
                col = (tok_pos ^ j) * own_cols
                out_ref[i * own_cols : (i + 1) * own_cols, j * own_cols : (j + 1) * own_cols] = (
                    work_ref[
                        pl.ds(pl.multiple_of(row, PANEL), own_cols),
                        pl.ds(pl.multiple_of(col, PANEL), own_cols),
                    ]
                )


def inverse_factor(pieces, own_cols, rows_moved, scale):
    tok_count, gc_count, rows, rank = pieces.shape
    tok_pos, gc_pos = lax.axis_index("tok"), lax.axis_index("gc")
    aligned = own_cols % PANEL == 0 and rows % SUB == 0
    moved = (
        (tok_pos ^ jnp.arange(tok_count, dtype=jnp.int32))[:, None] * own_cols
        + jnp.arange(own_cols, dtype=jnp.int32)[None, :]
    ).reshape(rank)
    if aligned:
        pos = jnp.stack([tok_pos, gc_pos]).astype(jnp.int32)
    else:
        pos = jnp.zeros((2,), jnp.int32)
        order = (
            (tok_pos ^ jnp.arange(tok_count, dtype=jnp.int32))[:, None] * gc_count
            + (gc_pos ^ jnp.arange(gc_count, dtype=jnp.int32))[None, :]
        ).reshape(-1)
        place = (order[:, None] * rows + jnp.arange(rows, dtype=jnp.int32)[None, :]).reshape(rank)
        full = jnp.zeros((rank, rank), jnp.float32).at[place].set(pieces.reshape(rank, rank))
        pieces = full.reshape(1, 1, rank, rank)
    inverse = pl.pallas_call(
        functools.partial(factor_kernel, scale, own_cols if aligned else rank, rows_moved),
        out_shape=jax.ShapeDtypeStruct((rank, rank), jnp.float32),
        in_specs=[
            pl.BlockSpec(memory_space=pltpu.SMEM),
            pl.BlockSpec(memory_space=pltpu.VMEM),
        ],
        out_specs=pl.BlockSpec(memory_space=pltpu.VMEM),
        scratch_shapes=[
            pltpu.VMEM((rank, rank), jnp.float32),
            pltpu.VMEM((PANEL, PANEL), jnp.float32),
        ],
        compiler_params=pltpu.CompilerParams(vmem_limit_bytes=32 * 1024 * 1024),
        name="inverse_factor",
    )(pos, pieces)
    if not aligned:
        inverse = jnp.take(inverse, moved, axis=1)
        if rows_moved:
            inverse = jnp.take(inverse, moved, axis=0)
    return inverse


def split(value):
    high = lax.reduce_precision(value, 8, 7)
    return high.astype(jnp.bfloat16), (value - high).astype(jnp.bfloat16)


def swap(value, axis, k):
    if k == 0:
        return value
    return lax.ppermute(value, axis, [(i, i ^ k) for i in range(lax.axis_size(axis))])


def collect(value, axis):
    return [swap(value, axis, k) for k in range(lax.axis_size(axis))]


def per_device(acts, init_basis, kept, member):
    owned = init_basis.shape[0]
    slice_rows = init_basis.shape[1]
    rank = init_basis.shape[2]
    tok_count = lax.axis_size("tok")
    gr_count = lax.axis_size("gr")
    gc_count = lax.axis_size("gc")
    block_cols = slice_rows * tok_count
    tok_rows = acts.shape[0]
    total_tokens = tok_rows * tok_count
    groups = kept.shape[0] // GBLK
    assert groups == gr_count == 2
    group_cols = GBLK * block_cols
    own_cols = rank // tok_count
    tok_pos = lax.axis_index("tok")
    gr_pos = lax.axis_index("gr")
    gc_pos = lax.axis_index("gc")
    first = (gr_pos * gc_count + gc_pos) * owned
    links = ((member[:, None] == member[None, :]).astype(jnp.int32) * kept).astype(jnp.float32)
    own_links = lax.dynamic_slice_in_dim(links, first, owned, 0)
    own_groups = lax.dynamic_slice_in_dim(member, first, owned, 0)

    def columns_of(array, k):
        return lax.dynamic_slice_in_dim(
            array, (tok_pos ^ k) * own_cols, own_cols, array.ndim - 1
        )

    init_bf = init_basis.astype(jnp.bfloat16)
    slices = [swap(columns_of(init_bf, k), "tok", k) for k in range(tok_count)]
    own_basis = jnp.concatenate(
        [lax.select_n(tok_pos ^ a, *slices) for a in range(tok_count)], axis=1
    )
    full_x = jnp.concatenate(collect(acts, "tok"), axis=0).reshape(
        total_tokens, owned, block_cols
    )
    basis_bf = lax.all_gather(init_bf, "tok", axis=1, tiled=True)
    basis_bf = jnp.concatenate([columns_of(basis_bf, k) for k in range(tok_count)], axis=2)

    def mix(own_basis):
        proj = jnp.einsum(
            "tob,obr->otr", full_x, own_basis, preferred_element_type=jnp.float32
        ).astype(jnp.bfloat16)
        total = jnp.zeros(proj.shape, jnp.float32)
        for b, near in enumerate(collect(proj, "gc")):
            for a, piece in enumerate(collect(near, "gr")):
                source = ((gr_pos ^ a) * gc_count + (gc_pos ^ b)) * owned
                weights = lax.dynamic_slice_in_dim(own_links, source, owned, 1)
                for j in range(owned):
                    total += weights[:, j][:, None, None] * piece[j][None].astype(jnp.float32)
        return total.astype(jnp.bfloat16)

    def gather_mixed(mixed):
        blocks = mixed.reshape(owned, tok_count, tok_rows, own_cols)
        pieces = []
        for k, piece in enumerate(collect(blocks, "tok")):
            pieces.append(
                jnp.concatenate([piece[:, i ^ k : (i ^ k) + 1] for i in range(tok_count)], axis=1)
            )
        return jnp.concatenate(pieces, axis=3).reshape(owned, total_tokens, rank)

    def factor(image, rows_moved):
        grams = jnp.einsum("obr,obs->ors", image[:, :, :own_cols], image, precision=HIGHEST)

        def group_sum(g):
            mask = (own_groups == g).astype(jnp.float32)
            return jnp.sum(mask[:, None, None] * grams, axis=0)

        total = group_sum(gr_pos) + swap(group_sum(gr_pos ^ 1), "gr", 1)
        rows = own_cols // gc_count

        def rows_of(i):
            return lax.dynamic_slice_in_dim(total, (gc_pos ^ i) * rows, rows, 0)

        piece = sum(swap(rows_of(i), "gc", i) for i in range(gc_count))
        blocks = [piece[:, k * own_cols : (k + 1) * own_cols] for k in range(tok_count)]
        piece = jnp.concatenate(
            [lax.select_n(tok_pos ^ a, *blocks) for a in range(tok_count)], axis=1
        )
        near = jnp.stack(collect(piece, "gc"))
        pieces = jnp.stack(collect(near, "tok"))
        own = inverse_factor(pieces, own_cols, rows_moved, 1.0 / group_cols)
        other = swap(own, "gr", 1)
        of_block = jnp.stack(
            [jnp.where(own_groups[o] == gr_pos, own, other) for o in range(owned)]
        )
        of_group = [jnp.where(gr_pos == g, own, other) for g in range(groups)]
        return of_block, of_group

    for step in range(ITERS):
        mixed = gather_mixed(mix(own_basis))
        cover = jnp.einsum("tob,otr->obr", full_x, mixed, preferred_element_type=jnp.float32)
        image = cover / total_tokens + ridge * basis_bf.astype(jnp.float32)
        of_block, of_group = factor(image, step < ITERS - 1)
        if step < ITERS - 1:
            basis_bf = jnp.einsum("obr,osr->obs", image, of_block, precision=HIGHEST).astype(
                jnp.bfloat16
            )
            own_basis = basis_bf[:, :, :own_cols]
    rows = lax.dynamic_slice_in_dim(image, tok_pos * slice_rows, slice_rows, 1)
    basis = jnp.einsum("obr,osr->obs", rows, of_block, precision=HIGHEST)
    own_x = acts.reshape(tok_rows, owned, block_cols)
    codes = sum(
        jnp.einsum("tob,obr->otr", own_x, part, preferred_element_type=jnp.float32)
        for part in split(image)
    )
    placed = jnp.concatenate(
        [
            jnp.sum((own_groups == g).astype(jnp.float32)[:, None, None] * codes, axis=0)
            for g in range(groups)
        ],
        axis=1,
    )
    placed = lax.psum_scatter(placed, ("gr", "gc"), scatter_dimension=0, tiled=True)
    latent = jnp.concatenate(
        [
            jnp.einsum(
                "tr,sr->ts",
                placed[:, g * rank : (g + 1) * rank],
                of_group[g],
                precision=HIGHEST,
            )
            for g in range(groups)
        ],
        axis=1,
    )
    latent = latent * (1.0 / math.sqrt(group_cols))
    return (basis, latent.astype(jnp.bfloat16))


def solution(mesh):
    placed = (P("tok", ("gr", "gc")), P(("gr", "gc"), "tok", None), P(), P())
    return jax.shard_map(
        per_device,
        mesh=mesh,
        in_specs=placed,
        out_specs=(P(("gr", "gc"), "tok", None), P(("tok", "gr", "gc"), None)),
        check_vma=False,
    )
```

time: 571 us -> 349 us (0.61)
  waiting for transfers between devices: 377 us -> 129 us
  starting transfers between devices: 0.91 us -> 57.9 us
  matrix products: 45.9 us -> 26.4 us
  Pallas kernels: 108 us -> 95.5 us
  other arithmetic: 5.02 us -> 11.8 us
    all_gather x8 -> x1, waiting for transfers between devices: 312 us -> 0.02 us  [per_device(): basis_bf = lax.all_gather(init_bf, 'tok', axis=1, tiled=True)]
    ppermute x0 -> x48, waiting for transfers between devices: none -> 129 us  [swap(): lax.ppermute(value, axis, [(i, i ^ k) for i in range(lax.axis_size(axis))])]
    reduce_scatter x2 -> x0, waiting for transfers between devices: 65.3 us -> none  [per_device(): lax.psum_scatter(stacked, ('gr', 'gc'), scatter_dimension=1, tiled=True)]
    ppermute x0 -> x48, starting transfers between devices: none -> 57.8 us  [swap(): lax.ppermute(value, axis, [(i, i ^ k) for i in range(lax.axis_size(axis))])]
    dot_general x10 -> x8, matrix products: 35.1 us -> 21.5 us  [the longest x1 7.28 us: per_device(): jnp.einsum('obr,osr->obs', image, of_block, precision=HIGHEST)]
    pallas_call x2, Pallas kernels: 108 us -> 95.5 us  [inverse_factor(): pl.pallas_call(functools.partial(factor_kernel, scale, own_cols if aligne...]
    unnamed x25 -> x18, local copies, waits for them, and re-layouts: 10.9 us -> 3.13 us
  transfers between devices with their start and end apart: 11 -> 50, of which waited for: 10 -> 27; matrix products, arithmetic and copies ran while one was open for 1% -> 4% of each run, Pallas kernels for 10% -> 14%
where the time goes in v2:
time: 349 us; the launch traced here: 344 us
  waiting for transfers between devices  129 us (37%)
  Pallas kernels  95.5 us (27%)
  starting transfers between devices  57.9 us (17%)
  matrix products  26.4 us (8%)
  between operations  16.6 us (5%)
  other arithmetic  11.8 us (3%)
  local copies, waits for them, and re-layouts  7.65 us (2%)
    ppermute x48, waiting for transfers between devices, swap(): lax.ppermute(value, axis, [(i, i ^ k) for i in range(lax.axis_size(axis))])  129 us
    pallas_call x2, Pallas kernels, inverse_factor(): pl.pallas_call(functools.partial(factor_kernel, scale, own_cols if aligne...  95.5 us
    ppermute x48, starting transfers between devices, swap(): lax.ppermute(value, axis, [(i, i ^ k) for i in range(lax.axis_size(axis))])  57.8 us
    dot_general x1, matrix products, per_device(): jnp.einsum('obr,osr->obs', image, of_block, precision=HIGHEST)  7.28 us
  transfers between devices with their start and end apart: 50, of which 27 were waited for; matrix products, arithmetic and copies ran while one was open for 4% of the time, Pallas kernels for 14%

profile of v2, /device:TPU:0, one launch (start us, length us, event | category | flops | bytes accessed | tf_op | source)
XLA Modules:
  0.0 344.4 jit_solution(5611488183329675192)
XLA Ops:
  8.5 3.0 collective-permute-start
  20.4 22.8 %collective-permute-done.3 = bf16[2,256,128]{2,1,0:T(8,128)(2,1)S(1)} collective-permute-done((bf16[2,256,128]{2,1,0:T(8,128)(2,1)S(1)}, bf16[2,256,128]{2,1,0:T(8,128)(2,1)S(1)}, u32[]{:S(2)}, u32[]{:S(2)}) %collective-permute-start.3) | collective-permute-done | bytes 131104 | tf_op jit(solution)/shard_map/ppermute | solution.py:147
  43.2 2.7 collective-permute-start.5
  46.4 2.7 collective-permute-done.5
  58.2 5.3 %collective-permute-done.7 = bf16[2,512,128]{2,1,0:T(8,128)(2,1)S(1)} collective-permute-done((bf16[2,512,128]{2,1,0:T(8,128)(2,1)S(1)}, bf16[2,512,128]{2,1,0:T(8,128)(2,1)S(1)}, u32[]{:S(2)}, u32[]{:S(2)}) %collective-permute-start.7) | collective-permute-done | bytes 262176 | tf_op jit(solution)/shard_map/ppermute | solution.py:147
  63.6 12.6 %collective-permute-done.9 = bf16[2,512,128]{2,1,0:T(8,128)(2,1)S(1)} collective-permute-done((bf16[2,512,128]{2,1,0:T(8,128)(2,1)S(1)}, bf16[2,512,128]{2,1,0:T(8,128)(2,1)S(1)}, u32[]{:S(2)}, u32[]{:S(2)}) %collective-permute-start.9) | collective-permute-done | bytes 262176 | tf_op jit(solution)/shard_map/ppermute | solution.py:147
  83.0 11.2 %collective-permute-done.14 = bf16[2,4,128,128]{3,2,1,0:T(8,128)(2,1)S(1)} collective-permute-done((bf16[2,4,128,128]{3,2,1,0:T(8,128)(2,1)S(1)}, bf16[2,4,128,128]{3,2,1,0:T(8,128)(2,1)S(1)}, u32[]{:S(2)}, u32[]{:S(2)}) %collective-permute-start.14) | collective-permute-done | bytes 262176 | tf_op jit(solution)/shard_map/ppermute | solution.py:147
  97.9 2.8 multiply_reduce_fusion.4
  102.4 3.0 collective-permute-start.17
  107.9 5.8 %collective-permute-done.18 = f32[32,512]{1,0:T(8,128)S(1)} collective-permute-done((f32[32,512]{1,0:T(8,128)S(1)}, f32[32,512]{1,0:T(8,128)S(1)}, u32[]{:S(2)}, u32[]{:S(2)}) %collective-permute-start.18) | collective-permute-done | bytes 65568 | tf_op jit(solution)/shard_map/ppermute | solution.py:147
  118.7 4.1 %collective-permute-done.21 = f32[32,512]{1,0:T(8,128)S(1)} collective-permute-done((f32[32,512]{1,0:T(8,128)S(1)}, f32[32,512]{1,0:T(8,128)S(1)}, u32[]{:S(2)}, u32[]{:S(2)}) %collective-permute-start.21) | collective-permute-done | bytes 65568 | tf_op jit(solution)/shard_map/ppermute | solution.py:147
  126.4 5.7 %collective-permute-done.23 = f32[4,32,512]{2,1,0:T(8,128)S(1)} collective-permute-done((f32[4,32,512]{2,1,0:T(8,128)S(1)}, f32[4,32,512]{2,1,0:T(8,128)S(1)}, u32[]{:S(2)}, u32[]{:S(2)}) %collective-permute-start.23) | collective-permute-done | bytes 262176 | tf_op jit(solution)/shard_map/ppermute | solution.py:147
  136.1 47.6 %inverse_factor.2 = f32[512,512]{1,0:T(8,128)S(1)} custom-call(s32[2]{0:T(128)S(1)} %pad_add_fusion.pos_ref, f32[4,4,32,512]{3,2,1,0:T(8,128)S(1)} %pad_maximum_fusion.1.pieces_ref), custom_call_target="tpu_custom_call" | custom-call | tf_op jit(solution)/shard_map/inverse_factor/pallas_call | solution.py:117
  188.4 7.3 %fusion.12 = bf16[2,1024,512]{2,1,0:T(8,128)(2,1)S(1)} fusion(f32[2,1024,512]{2,1,0:T(8,128)S(1)} %copy-done.2, f32[1,512,512]{2,1,0:T(8,128)S(1)} %get-tuple-element.29, f32[1,512,512]{2,1,0:T(8,128)S(1)} %get-tuple-element.28), kind=kOutput, calls=%fused_computation.16 | convolution fusion | flops 6444023808 | bytes 8388608 | tf_op jit(solution)/shard_map/obr,osr->obs/dot_general | solution.py:248
  201.2 9.4 %collective-permute-done.28 = bf16[2,512,128]{2,1,0:T(8,128)(2,1)S(1)} collective-permute-done((bf16[2,512,128]{2,1,0:T(8,128)(2,1)S(1)}, bf16[2,512,128]{2,1,0:T(8,128)(2,1)S(1)}, u32[]{:S(2)}, u32[]{:S(2)}) %collective-permute-start.28) | collective-permute-done | bytes 262176 | tf_op jit(solution)/shard_map/ppermute | solution.py:147
  210.7 8.4 %collective-permute-done.30 = bf16[2,512,128]{2,1,0:T(8,128)(2,1)S(1)} collective-permute-done((bf16[2,512,128]{2,1,0:T(8,128)(2,1)S(1)}, bf16[2,512,128]{2,1,0:T(8,128)(2,1)S(1)}, u32[]{:S(2)}, u32[]{:S(2)}) %collective-permute-start.30) | collective-permute-done | bytes 262176 | tf_op jit(solution)/shard_map/ppermute | solution.py:147
  225.9 10.5 %collective-permute-done.35 = bf16[2,4,128,128]{3,2,1,0:T(8,128)(2,1)S(1)} collective-permute-done((bf16[2,4,128,128]{3,2,1,0:T(8,128)(2,1)S(1)}, bf16[2,4,128,128]{3,2,1,0:T(8,128)(2,1)S(1)}, u32[]{:S(2)}, u32[]{:S(2)}) %collective-permute-start.35) | collective-permute-done | bytes 262176 | tf_op jit(solution)/shard_map/ppermute | solution.py:147
  237.9 2.8 multiply_reduce_fusion.2
  242.3 4.7 %collective-permute-start.38 = (f32[32,512]{1,0:T(8,128)S(1)}, f32[32,512]{1,0:T(8,128)S(1)}, u32[]{:S(2)}, u32[]{:S(2)}) collective-permute-start(f32[32,512]{1,0:T(8,128)S(1)} %get-tuple-element.43), channel_id=1, source_target_pairs={{0,1},{1,0},{2,3},{3,2},{4,5},{5,4},{6,7},{7,6},{8,9},{9,8},{10,11... | collective-permute-start | bytes 196616 | tf_op jit(solution)/shard_map/ppermute | solution.py:147
  250.3 4.9 %collective-permute-done.39 = f32[32,512]{1,0:T(8,128)S(1)} collective-permute-done((f32[32,512]{1,0:T(8,128)S(1)}, f32[32,512]{1,0:T(8,128)S(1)}, u32[]{:S(2)}, u32[]{:S(2)}) %collective-permute-start.39) | collective-permute-done | bytes 65568 | tf_op jit(solution)/shard_map/ppermute | solution.py:147
  260.8 4.5 %collective-permute-done.42 = f32[32,512]{1,0:T(8,128)S(1)} collective-permute-done((f32[32,512]{1,0:T(8,128)S(1)}, f32[32,512]{1,0:T(8,128)S(1)}, u32[]{:S(2)}, u32[]{:S(2)}) %collective-permute-start.42) | collective-permute-done | bytes 65568 | tf_op jit(solution)/shard_map/ppermute | solution.py:147
  270.9 3.8 %collective-permute-done.44 = f32[4,32,512]{2,1,0:T(8,128)S(1)} collective-permute-done((f32[4,32,512]{2,1,0:T(8,128)S(1)}, f32[4,32,512]{2,1,0:T(8,128)S(1)}, u32[]{:S(2)}, u32[]{:S(2)}) %collective-permute-start.44) | collective-permute-done | bytes 262176 | tf_op jit(solution)/shard_map/ppermute | solution.py:147
  278.8 47.9 %inverse_factor.3 = f32[512,512]{1,0:T(8,128)S(1)} custom-call(s32[2]{0:T(128)S(1)} %pad_add_fusion.pos_ref, f32[4,4,32,512]{3,2,1,0:T(8,128)S(1)} %pad_maximum_fusion.2.pieces_ref), custom_call_target="tpu_custom_call" | custom-call | tf_op jit(solution)/shard_map/inverse_factor/pallas_call | solution.py:117
  332.9 4.1 %fusion.8 = f32[2,256,512]{2,1,0:T(8,128)} fusion(f32[1,512,512]{2,1,0:T(8,128)S(1)} %get-tuple-element.27, f32[1,512,512]{2,1,0:T(8,128)S(1)} %get-tuple-element.26, f32[2,1024,512]{2,1,0:T(8,128)} %copy-done, s32[]{:T(128)S(6)} %select_n.459), kind=kOutput, calls=%fused_computation.12 | convolution fusion | flops 1611137024 | bytes 4194308 | tf_op jit(solution)/shard_map/obr,osr->obs/dot_general | solution.py:253
  (177 shorter events, 90.1 us)
Async XLA Ops:
  7.2 87.3 %all-gather.2.cloned.1.call-start = ((), (), s32[]{:S(2)}) async-start(), calls=%async_computation.1 | async-start | bytes 2621440 | tf_op jit(solution)/shard_map/all_gather | solution.py:189
  8.5 41.6 %collective-permute-start = (bf16[128,2048]{0,1:T(8,128)(2,1)S(1)}, bf16[128,2048]{0,1:T(8,128)(2,1)S(1)}, u32[]{:S(2)}, u32[]{:S(2)}) collective-permute-start(bf16[128,2048]{0,1:T(8,128)(2,1)S(1)} %copy.29), channel_id=1, source_target_pairs={{0,8},{8,0},{16,24},{24,16},{1,9},{9,1},{17,25},{25,17},{2,10},{10... | collective-permute-start | bytes 1572872 | tf_op jit(solution)/shard_map/ppermute | solution.py:147
  11.6 38.6 %collective-permute-start.1 = (bf16[128,2048]{0,1:T(8,128)(2,1)S(1)}, bf16[128,2048]{0,1:T(8,128)(2,1)S(1)}, u32[]{:S(2)}, u32[]{:S(2)}) collective-permute-start(bf16[128,2048]{0,1:T(8,128)(2,1)S(1)} %copy.29), channel_id=1, source_target_pairs={{0,16},{8,24},{16,0},{24,8},{1,17},{9,25},{17,1},{25,9},{2,18},{10... | collective-permute-start | bytes 1572872 | tf_op jit(solution)/shard_map/ppermute | solution.py:147
  13.1 37.9 %collective-permute-start.2 = (bf16[128,2048]{0,1:T(8,128)(2,1)S(1)}, bf16[128,2048]{0,1:T(8,128)(2,1)}, u32[]{:S(2)}, u32[]{:S(2)}) collective-permute-start(bf16[128,2048]{0,1:T(8,128)(2,1)S(1)} %copy.29), channel_id=1, source_target_pairs={{0,24},{8,16},{16,8},{24,0},{1,25},{9,17},{17,9},{25,1},{2,26},{10... | collective-permute-start | bytes 1572872 | tf_op jit(solution)/shard_map/ppermute | solution.py:147
  15.2 311.6 %reduce-scatter.4.cloned.1.call-start = ((), (), s32[]{:S(2)}) async-start(), calls=%async_computation.2 | async-start | bytes 589824
  16.4 26.8 %collective-permute-start.3 = (bf16[2,256,128]{2,1,0:T(8,128)(2,1)S(1)}, bf16[2,256,128]{2,1,0:T(8,128)(2,1)S(1)}, u32[]{:S(2)}, u32[]{:S(2)}) collective-permute-start(bf16[2,256,128]{2,1,0:T(8,128)(2,1)S(1)} %get-tuple-element.38), channel_id=1, source_target_pairs={{0,8},{8,0},{16,24},{24,16},{1,9},{9,1},{17,25},{25,17},{2,10},{10... | collective-permute-start | bytes 393224 | tf_op jit(solution)/shard_map/ppermute | solution.py:147
  18.4 28.0 %collective-permute-start.4 = (bf16[2,256,128]{2,1,0:T(8,128)(2,1)S(1)}, bf16[2,256,128]{2,1,0:T(8,128)(2,1)S(1)}, u32[]{:S(2)}, u32[]{:S(2)}) collective-permute-start(bf16[2,256,128]{2,1,0:T(8,128)(2,1)S(1)} %get-tuple-element.40), channel_id=1, source_target_pairs={{0,16},{8,24},{16,0},{24,8},{1,17},{9,25},{17,1},{25,9},{2,18},{10... | collective-permute-start | bytes 393224 | tf_op jit(solution)/shard_map/ppermute | solution.py:147
  55.4 20.8 %collective-permute-start.9 = (bf16[2,512,128]{2,1,0:T(8,128)(2,1)S(1)}, bf16[2,512,128]{2,1,0:T(8,128)(2,1)S(1)}, u32[]{:S(2)}, u32[]{:S(2)}) collective-permute-start(bf16[2,512,128]{2,1,0:T(8,128)(2,1)S(1)} %convolution_convert_fusion.1), channel_id=1, source_target_pairs={{0,2},{1,3},{2,0},{3,1},{4,6},{5,7},{6,4},{7,5},{8,10},{9,11},{10,... | collective-permute-start | bytes 786440 | tf_op jit(solution)/shard_map/ppermute | solution.py:147
  58.1 18.2 %collective-permute-start.11 = (bf16[2,512,128]{2,1,0:T(8,128)(2,1)S(1)}, bf16[2,512,128]{2,1,0:T(8,128)(2,1)S(1)}, u32[]{:S(2)}, u32[]{:S(2)}) collective-permute-start(bf16[2,512,128]{2,1,0:T(8,128)(2,1)S(1)} %convolution_convert_fusion.1), channel_id=1, source_target_pairs={{0,3},{1,2},{2,1},{3,0},{4,7},{5,6},{6,5},{7,4},{8,11},{9,10},{10,... | collective-permute-start | bytes 786440 | tf_op jit(solution)/shard_map/ppermute | solution.py:147
  58.1 18.9 %collective-permute-start.6 = (bf16[2,512,128]{2,1,0:T(8,128)(2,1)S(1)}, bf16[2,512,128]{2,1,0:T(8,128)(2,1)S(1)}, u32[]{:S(2)}, u32[]{:S(2)}) collective-permute-start(bf16[2,512,128]{2,1,0:T(8,128)(2,1)S(1)} %convolution_convert_fusion.1), channel_id=1, source_target_pairs={{0,4},{4,0},{1,5},{5,1},{2,6},{6,2},{3,7},{7,3},{8,12},{12,8},{9,1... | collective-permute-start | bytes 786440 | tf_op jit(solution)/shard_map/ppermute | solution.py:147
  63.5 13.6 %collective-permute-start.8 = (bf16[2,512,128]{2,1,0:T(8,128)(2,1)S(1)}, bf16[2,512,128]{2,1,0:T(8,128)(2,1)S(1)}, u32[]{:S(2)}, u32[]{:S(2)}) collective-permute-start(bf16[2,512,128]{2,1,0:T(8,128)(2,1)S(1)} %collective-permute-done.7), channel_id=1, source_target_pairs={{0,4},{4,0},{1,5},{5,1},{2,6},{6,2},{3,7},{7,3},{8,12},{12,8},{9,1... | collective-permute-start | bytes 786440 | tf_op jit(solution)/shard_map/ppermute | solution.py:147
  78.9 15.4 %collective-permute-start.13 = (bf16[2,4,128,128]{3,2,1,0:T(8,128)(2,1)S(1)}, bf16[2,4,128,128]{3,2,1,0:T(8,128)(2,1)S(1)}, u32[]{:S(2)}, u32[]{:S(2)}) collective-permute-start(bf16[2,4,128,128]{3,2,1,0:T(8,128)(2,1)S(1)} %add_convert_fusion.2), channel_id=1, source_target_pairs={{0,8},{8,0},{16,24},{24,16},{1,9},{9,1},{17,25},{25,17},{2,10},{10... | collective-permute-start | bytes 786440 | tf_op jit(solution)/shard_map/ppermute | solution.py:147
  80.4 13.8 %collective-permute-start.14 = (bf16[2,4,128,128]{3,2,1,0:T(8,128)(2,1)S(1)}, bf16[2,4,128,128]{3,2,1,0:T(8,128)(2,1)S(1)}, u32[]{:S(2)}, u32[]{:S(2)}) collective-permute-start(bf16[2,4,128,128]{3,2,1,0:T(8,128)(2,1)S(1)} %add_convert_fusion.2), channel_id=1, source_target_pairs={{0,16},{8,24},{16,0},{24,8},{1,17},{9,25},{17,1},{25,9},{2,18},{10... | collective-permute-start | bytes 786440 | tf_op jit(solution)/shard_map/ppermute | solution.py:147
  81.9 12.5 %collective-permute-start.15 = (bf16[2,4,128,128]{3,2,1,0:T(8,128)(2,1)S(1)}, bf16[2,4,128,128]{3,2,1,0:T(8,128)(2,1)S(1)}, u32[]{:S(2)}, u32[]{:S(2)}) collective-permute-start(bf16[2,4,128,128]{3,2,1,0:T(8,128)(2,1)S(1)} %add_convert_fusion.2), channel_id=1, source_target_pairs={{0,24},{8,16},{16,8},{24,0},{1,25},{9,17},{17,9},{25,1},{2,26},{10... | collective-permute-start | bytes 786440 | tf_op jit(solution)/shard_map/ppermute | solution.py:147
  124.9 11.1 %collective-permute-start.25 = (f32[4,32,512]{2,1,0:T(8,128)S(1)}, f32[4,32,512]{2,1,0:T(8,128)S(1)}, u32[]{:S(2)}, u32[]{:S(2)}) collective-permute-start(f32[4,32,512]{2,1,0:T(8,128)S(1)} %get-tuple-element.89), channel_id=1, source_target_pairs={{0,24},{8,16},{16,8},{24,0},{1,25},{9,17},{17,9},{25,1},{2,26},{10... | collective-permute-start | bytes 786440 | tf_op jit(solution)/shard_map/ppermute | solution.py:147
  196.7 13.9 %collective-permute-start.28 = (bf16[2,512,128]{2,1,0:T(8,128)(2,1)S(1)}, bf16[2,512,128]{2,1,0:T(8,128)(2,1)S(1)}, u32[]{:S(2)}, u32[]{:S(2)}) collective-permute-start(bf16[2,512,128]{2,1,0:T(8,128)(2,1)S(1)} %convolution_convert_fusion), channel_id=1, source_target_pairs={{0,1},{1,0},{2,3},{3,2},{4,5},{5,4},{6,7},{7,6},{8,9},{9,8},{10,11... | collective-permute-start | bytes 786440 | tf_op jit(solution)/shard_map/ppermute | solution.py:147
  197.8 21.3 %collective-permute-start.30 = (bf16[2,512,128]{2,1,0:T(8,128)(2,1)S(1)}, bf16[2,512,128]{2,1,0:T(8,128)(2,1)S(1)}, u32[]{:S(2)}, u32[]{:S(2)}) collective-permute-start(bf16[2,512,128]{2,1,0:T(8,128)(2,1)S(1)} %convolution_convert_fusion), channel_id=1, source_target_pairs={{0,2},{1,3},{2,0},{3,1},{4,6},{5,7},{6,4},{7,5},{8,10},{9,11},{10,... | collective-permute-start | bytes 786440 | tf_op jit(solution)/shard_map/ppermute | solution.py:147
  199.6 19.6 %collective-permute-start.32 = (bf16[2,512,128]{2,1,0:T(8,128)(2,1)S(1)}, bf16[2,512,128]{2,1,0:T(8,128)(2,1)S(1)}, u32[]{:S(2)}, u32[]{:S(2)}) collective-permute-start(bf16[2,512,128]{2,1,0:T(8,128)(2,1)S(1)} %convolution_convert_fusion), channel_id=1, source_target_pairs={{0,3},{1,2},{2,1},{3,0},{4,7},{5,6},{6,5},{7,4},{8,11},{9,10},{10,... | collective-permute-start | bytes 786440 | tf_op jit(solution)/shard_map/ppermute | solution.py:147
  201.1 18.7 %collective-permute-start.27 = (bf16[2,512,128]{2,1,0:T(8,128)(2,1)S(1)}, bf16[2,512,128]{2,1,0:T(8,128)(2,1)S(1)}, u32[]{:S(2)}, u32[]{:S(2)}) collective-permute-start(bf16[2,512,128]{2,1,0:T(8,128)(2,1)S(1)} %convolution_convert_fusion), channel_id=1, source_target_pairs={{0,4},{4,0},{1,5},{5,1},{2,6},{6,2},{3,7},{7,3},{8,12},{12,8},{9,1... | collective-permute-start | bytes 786440 | tf_op jit(solution)/shard_map/ppermute | solution.py:147
  221.7 14.7 %collective-permute-start.34 = (bf16[2,4,128,128]{3,2,1,0:T(8,128)(2,1)S(1)}, bf16[2,4,128,128]{3,2,1,0:T(8,128)(2,1)S(1)}, u32[]{:S(2)}, u32[]{:S(2)}) collective-permute-start(bf16[2,4,128,128]{3,2,1,0:T(8,128)(2,1)S(1)} %add_convert_fusion), channel_id=1, source_target_pairs={{0,8},{8,0},{16,24},{24,16},{1,9},{9,1},{17,25},{25,17},{2,10},{10... | collective-permute-start | bytes 786440 | tf_op jit(solution)/shard_map/ppermute | solution.py:147
  222.5 13.8 %collective-permute-start.35 = (bf16[2,4,128,128]{3,2,1,0:T(8,128)(2,1)S(1)}, bf16[2,4,128,128]{3,2,1,0:T(8,128)(2,1)S(1)}, u32[]{:S(2)}, u32[]{:S(2)}) collective-permute-start(bf16[2,4,128,128]{3,2,1,0:T(8,128)(2,1)S(1)} %add_convert_fusion), channel_id=1, source_target_pairs={{0,16},{8,24},{16,0},{24,8},{1,17},{9,25},{17,1},{25,9},{2,18},{10... | collective-permute-start | bytes 786440 | tf_op jit(solution)/shard_map/ppermute | solution.py:147
  224.0 12.4 %collective-permute-start.36 = (bf16[2,4,128,128]{3,2,1,0:T(8,128)(2,1)S(1)}, bf16[2,4,128,128]{3,2,1,0:T(8,128)(2,1)S(1)}, u32[]{:S(2)}, u32[]{:S(2)}) collective-permute-start(bf16[2,4,128,128]{3,2,1,0:T(8,128)(2,1)S(1)} %add_convert_fusion), channel_id=1, source_target_pairs={{0,24},{8,16},{16,8},{24,0},{1,25},{9,17},{17,9},{25,1},{2,26},{10... | collective-permute-start | bytes 786440 | tf_op jit(solution)/shard_map/ppermute | solution.py:147
  266.6 10.5 %collective-permute-start.45 = (f32[4,32,512]{2,1,0:T(8,128)S(1)}, f32[4,32,512]{2,1,0:T(8,128)S(1)}, u32[]{:S(2)}, u32[]{:S(2)}) collective-permute-start(f32[4,32,512]{2,1,0:T(8,128)S(1)} %get-tuple-element.42), channel_id=1, source_target_pairs={{0,16},{8,24},{16,0},{24,8},{1,17},{9,25},{17,1},{25,9},{2,18},{10... | collective-permute-start | bytes 786440 | tf_op jit(solution)/shard_map/ppermute | solution.py:147
  267.5 11.2 %collective-permute-start.46 = (f32[4,32,512]{2,1,0:T(8,128)S(1)}, f32[4,32,512]{2,1,0:T(8,128)S(1)}, u32[]{:S(2)}, u32[]{:S(2)}) collective-permute-start(f32[4,32,512]{2,1,0:T(8,128)S(1)} %get-tuple-element.42), channel_id=1, source_target_pairs={{0,24},{8,16},{16,8},{24,0},{1,25},{9,17},{17,9},{25,1},{2,26},{10... | collective-permute-start | bytes 786440 | tf_op jit(solution)/shard_map/ppermute | solution.py:147
  (34 other events, 239.0 us)
Sparse Core Ops, SparseCore 0:
  15.3 48.7 all-gather.1
  271.0 31.7 reduce-scatter.3

commit v3 on v2

--- a/solution.py
+++ b/solution.py
@@ -17,23 +17,61 @@
 HIGHEST = lax.Precision.HIGHEST
 
 
-def eliminate(tiles, store):
-    lane = lax.broadcasted_iota(jnp.int32, (1, PANEL), 1)
-    lane_tile = lax.broadcasted_iota(jnp.int32, (SUB, PANEL), 1)
+def reciprocal(value):
+    guess = pl.reciprocal(value, approx=True)
+    guess = guess * (2.0 - value * guess)
+    return guess * (2.0 - value * guess)
+
+
+def eliminate(tiles, inv_ref):
+    shape = (SUB, PANEL)
+    lane = lax.broadcasted_iota(jnp.int32, shape, 1)
+    sub = lax.broadcasted_iota(jnp.int32, shape, 0)
+
+    def spread(column):
+        return jnp.broadcast_to(column, shape)
+
     tiles = list(tiles)
-    for j in range(PANEL):
-        s, r = divmod(j, SUB)
-        row = tiles[s][r : r + 1, :]
-        pivot = row[:, j : j + 1]
-        unit = jnp.where(lane == j, 1.0, row)
-        root = lax.rsqrt(pivot)
-        root = root * (1.5 - 0.5 * pivot * root * root)
-        store(j, jnp.where(lane <= j, unit, 0.0) * root)
-        scaled = jnp.broadcast_to(unit * (1.0 / pivot), (SUB, PANEL))
-        first = s if r < SUB - 1 else s + 1
-        for q in range(first, PANEL // SUB):
-            factor = tiles[q][:, j : j + 1]
-            tiles[q] = jnp.where(lane_tile == j, 0.0, tiles[q]) - factor * scaled
+    for s in range(PANEL // SUB):
+        start = s * SUB
+        tile = tiles[s]
+        inside = (lane >= start) & (lane < start + SUB)
+        columns = [spread(tile[:, start + c : start + c + 1]) for c in range(SUB)]
+        pivot = [
+            [spread(columns[c][i : i + 1, :]) if c >= i else None for c in range(SUB)]
+            for i in range(SUB)
+        ]
+        base = jnp.where(inside, jnp.where(lane == start + sub, 1.0, 0.0), tile)
+        rows = [spread(base[i : i + 1, :]) for i in range(SUB)]
+        below = [[None] * SUB for _ in range(SUB)]
+        inverse = []
+        for b in range(SUB):
+            inverse.append(reciprocal(pivot[b][b]))
+            for i in range(b + 1, SUB):
+                factor = pivot[b][i] * inverse[b]
+                below[i][b] = factor
+                for c in range(i, SUB):
+                    pivot[i][c] = pivot[i][c] - factor * pivot[b][c]
+                rows[i] = rows[i] - factor * rows[b]
+        result = jnp.zeros(shape, jnp.float32)
+        for b in range(SUB):
+            root = lax.rsqrt(pivot[b][b])
+            root = root * (1.5 - 0.5 * pivot[b][b] * root * root)
+            result = jnp.where(sub == b, rows[b] * root, result)
+        inv_ref[start : start + SUB, :] = jnp.where(lane < start + SUB, result, 0.0)
+        solved = [None] * SUB
+        for b in reversed(range(SUB)):
+            value = rows[b] * inverse[b]
+            for i in reversed(range(b + 1, SUB)):
+                value = value - below[i][b] * solved[i]
+            solved[b] = value
+        for q in range(s + 1, PANEL // SUB):
+            parts = [
+                spread(tiles[q][:, start + b : start + b + 1]) * solved[b] for b in range(SUB)
+            ]
+            while len(parts) > 1:
+                parts = [x + y for x, y in zip(parts[::2], parts[1::2])]
+            tiles[q] = jnp.where(inside, 0.0, tiles[q]) - parts[0]
 
 
 def factor_kernel(scale, own_cols, rows_moved, pos_ref, pieces_ref, out_ref, work_ref, inv_ref):
@@ -49,10 +87,7 @@
         here = pl.ds(pl.multiple_of(k * PANEL, PANEL), PANEL)
         diag = work_ref[here, here]
 
-        def store(j, row):
-            inv_ref[j : j + 1, :] = row
-
-        eliminate([diag[SUB * q : SUB * (q + 1), :] for q in range(PANEL // SUB)], store)
+        eliminate([diag[SUB * q : SUB * (q + 1), :] for q in range(PANEL // SUB)], inv_ref)
         inv = inv_ref[...]
         work_ref[here, :] = jnp.dot(
             inv, work_ref[here, :], preferred_element_type=jnp.float32, precision=HIGHEST
@@ -183,10 +218,10 @@
     own_basis = jnp.concatenate(
         [lax.select_n(tok_pos ^ a, *slices) for a in range(tok_count)], axis=1
     )
-    full_x = jnp.concatenate(collect(acts, "tok"), axis=0).reshape(
-        total_tokens, owned, block_cols
-    )
-    basis_bf = lax.all_gather(init_bf, "tok", axis=1, tiled=True)
+    acts_pieces = collect(acts, "tok")
+    acts_pieces, init_late = lax.optimization_barrier((acts_pieces, init_bf))
+    full_x = jnp.concatenate(acts_pieces, axis=0).reshape(total_tokens, owned, block_cols)
+    basis_bf = lax.all_gather(init_late, "tok", axis=1, tiled=True)
     basis_bf = jnp.concatenate([columns_of(basis_bf, k) for k in range(tok_count)], axis=2)
 
     def mix(own_basis):
@@ -245,10 +280,13 @@
         image = cover / total_tokens + ridge * basis_bf.astype(jnp.float32)
         of_block, of_group = factor(image, step < ITERS - 1)
         if step < ITERS - 1:
-            basis_bf = jnp.einsum("obr,osr->obs", image, of_block, precision=HIGHEST).astype(
-                jnp.bfloat16
-            )
-            own_basis = basis_bf[:, :, :own_cols]
+            own_basis = jnp.einsum(
+                "obr,osr->obs", image, of_block[:, :own_cols], precision=HIGHEST
+            ).astype(jnp.bfloat16)
+            other_basis = jnp.einsum(
+                "obr,osr->obs", image, of_block[:, own_cols:], precision=HIGHEST
+            ).astype(jnp.bfloat16)
+            basis_bf = jnp.concatenate([own_basis, other_basis], axis=2)
     rows = lax.dynamic_slice_in_dim(image, tok_pos * slice_rows, slice_rows, 1)
     basis = jnp.einsum("obr,osr->obs", rows, of_block, precision=HIGHEST)
     own_x = acts.reshape(tok_rows, owned, block_cols)

time: 349 us -> 329 us (0.943)
  Pallas kernels: 95.5 us -> 63.5 us
  other arithmetic: 11.8 us -> 19.3 us
  local copies, waits for them, and re-layouts: 7.65 us -> 15 us
  starting transfers between devices: 57.9 us -> 51.8 us
  matrix products: 26.4 us -> 31.2 us
    pallas_call x2, Pallas kernels: 95.5 us -> 63.5 us  [inverse_factor(): pl.pallas_call(functools.partial(factor_kernel, scale, own_cols if aligne...]
    ppermute x48, starting transfers between devices: 57.8 us -> 51.7 us  [swap(): lax.ppermute(value, axis, [(i, i ^ k) for i in range(lax.axis_size(axis))])]
    mul x16, other arithmetic: 1.12 us -> 6.66 us  [mix(): total += weights[:, j][:, None, None] * piece[j][None].astype(jnp.float32)]
    unnamed x18 -> x62, local copies, waits for them, and re-layouts: 3.13 us -> 7.98 us
    dot_general x1 -> x2, matrix products: 7.28 us -> 10.4 us  [the longest x1 6.77 us: per_device(): jnp.einsum('obr,osr->obs', image, of_block[:, own_cols:], precision=HIGHEST)]
  transfers between devices with their start and end apart: 50 -> 50, of which waited for: 27 -> 28; matrix products, arithmetic and copies ran while one was open for 4% -> 9% of each run, Pallas kernels for 14% -> 10%
where the time goes in v3:
time: 329 us; the launch traced here: 323 us
  waiting for transfers between devices  126 us (38%)
  Pallas kernels  63.5 us (19%)
  starting transfers between devices  51.8 us (16%)
  matrix products  31.2 us (9%)
  other arithmetic  19.3 us (6%)
  between operations  16.5 us (5%)
  local copies, waits for them, and re-layouts  15 us (5%)
    ppermute x48, waiting for transfers between devices, swap(): lax.ppermute(value, axis, [(i, i ^ k) for i in range(lax.axis_size(axis))])  126 us
    pallas_call x2, Pallas kernels, inverse_factor(): pl.pallas_call(functools.partial(factor_kernel, scale, own_cols if aligne...  63.5 us
    ppermute x48, starting transfers between devices, swap(): lax.ppermute(value, axis, [(i, i ^ k) for i in range(lax.axis_size(axis))])  51.7 us
    unnamed x62, local copies, waits for them, and re-layouts  7.98 us
    dot_general x1, matrix products, per_device(): jnp.einsum('obr,osr->obs', image, of_block[:, own_cols:], precision=HIGHEST)  6.77 us
    mul x16, other arithmetic, mix(): total += weights[:, j][:, None, None] * piece[j][None].astype(jnp.float32)  6.66 us
  transfers between devices with their start and end apart: 50, of which 28 were waited for; matrix products, arithmetic and copies ran while one was open for 9% of the time, Pallas kernels for 10%

profile of v3, /device:TPU:0, one launch (start us, length us, event | category | flops | bytes accessed | tf_op | source)
XLA Modules:
  0.0 323.2 jit_solution(4803343654485351508)
XLA Ops:
  8.6 3.0 collective-permute-start
  22.1 19.8 %collective-permute-done.4 = bf16[2,256,128]{2,1,0:T(8,128)(2,1)} collective-permute-done((bf16[2,256,128]{2,1,0:T(8,128)(2,1)S(1)}, bf16[2,256,128]{2,1,0:T(8,128)(2,1)}, u32[]{:S(2)}, u32[]{:S(2)}) %collective-permute-start.4) | collective-permute-done | bytes 131104 | tf_op jit(solution)/shard_map/ppermute | solution.py:182
  55.0 3.6 %collective-permute-start.11 = (bf16[2,512,128]{2,1,0:T(8,128)(2,1)}, bf16[2,512,128]{2,1,0:T(8,128)(2,1)}, u32[]{:S(2)}, u32[]{:S(2)}) collective-permute-start(bf16[2,512,128]{2,1,0:T(8,128)(2,1)} %convolution_convert_fusion.3), channel_id=1, source_target_pairs={{0,3},{1,2},{2,1},{3,0},{4,7},{5,6},{6,5},{7,4},{8,11},{9,10},{10,... | collective-permute-start | bytes 786440 | tf_op jit(solution)/shard_map/ppermute | solution.py:182
  61.5 4.9 %collective-permute-done.11 = bf16[2,512,128]{2,1,0:T(8,128)(2,1)} collective-permute-done((bf16[2,512,128]{2,1,0:T(8,128)(2,1)}, bf16[2,512,128]{2,1,0:T(8,128)(2,1)}, u32[]{:S(2)}, u32[]{:S(2)}) %collective-permute-start.11) | collective-permute-done | bytes 262176 | tf_op jit(solution)/shard_map/ppermute | solution.py:182
  67.5 11.3 %collective-permute-done.9 = bf16[2,512,128]{2,1,0:T(8,128)(2,1)} collective-permute-done((bf16[2,512,128]{2,1,0:T(8,128)(2,1)}, bf16[2,512,128]{2,1,0:T(8,128)(2,1)}, u32[]{:S(2)}, u32[]{:S(2)}) %collective-permute-start.9) | collective-permute-done | bytes 262176 | tf_op jit(solution)/shard_map/ppermute | solution.py:182
  87.8 16.7 %collective-permute-done.14 = bf16[2,4,128,128]{3,2,1,0:T(8,128)(2,1)S(1)} collective-permute-done((bf16[2,4,128,128]{3,2,1,0:T(8,128)(2,1)S(1)}, bf16[2,4,128,128]{3,2,1,0:T(8,128)(2,1)S(1)}, u32[]{:S(2)}, u32[]{:S(2)}) %collective-permute-start.14) | collective-permute-done | bytes 262176 | tf_op jit(solution)/shard_map/ppermute | solution.py:182
  104.6 3.7 %collective-permute-done.13 = bf16[2,4,128,128]{3,2,1,0:T(8,128)(2,1)S(1)} collective-permute-done((bf16[2,4,128,128]{3,2,1,0:T(8,128)(2,1)S(1)}, bf16[2,4,128,128]{3,2,1,0:T(8,128)(2,1)S(1)}, u32[]{:S(2)}, u32[]{:S(2)}) %collective-permute-start.13) | collective-permute-done | bytes 262176 | tf_op jit(solution)/shard_map/ppermute | solution.py:182
  114.6 2.8 multiply_reduce_fusion.4
  119.1 3.4 %collective-permute-start.19 = (f32[32,512]{1,0:T(8,128)S(1)}, f32[32,512]{1,0:T(8,128)S(1)}, u32[]{:S(2)}, u32[]{:S(2)}) collective-permute-start(f32[32,512]{1,0:T(8,128)S(1)} %get-tuple-element.101), channel_id=1, source_target_pairs={{0,3},{1,2},{2,1},{3,0},{4,7},{5,6},{6,5},{7,4},{8,11},{9,10},{10,... | collective-permute-start | bytes 196616 | tf_op jit(solution)/shard_map/ppermute | solution.py:182
  134.6 2.7 collective-permute-done.21
  141.0 6.6 %collective-permute-done.25 = f32[4,32,512]{2,1,0:T(8,128)S(1)} collective-permute-done((f32[4,32,512]{2,1,0:T(8,128)S(1)}, f32[4,32,512]{2,1,0:T(8,128)S(1)}, u32[]{:S(2)}, u32[]{:S(2)}) %collective-permute-start.25) | collective-permute-done | bytes 262176 | tf_op jit(solution)/shard_map/ppermute | solution.py:182
  147.6 4.0 %collective-permute-done.24 = f32[4,32,512]{2,1,0:T(8,128)S(1)} collective-permute-done((f32[4,32,512]{2,1,0:T(8,128)S(1)}, f32[4,32,512]{2,1,0:T(8,128)S(1)}, u32[]{:S(2)}, u32[]{:S(2)}) %collective-permute-start.24) | collective-permute-done | bytes 262176 | tf_op jit(solution)/shard_map/ppermute | solution.py:182
  151.9 31.8 %inverse_factor.2 = f32[512,512]{1,0:T(8,128)S(1)} custom-call(s32[2]{0:T(128)S(1)} %pad_add_fusion.pos_ref, f32[4,4,32,512]{3,2,1,0:T(8,128)S(1)} %pad_maximum_fusion.3.pieces_ref), custom_call_target="tpu_custom_call" | custom-call | tf_op jit(solution)/shard_map/inverse_factor/pallas_call | solution.py:152
  187.9 3.6 %convolution_convert_fusion.1 = bf16[2,1024,128]{2,1,0:T(8,128)(2,1)S(1)} fusion(f32[2,1024,512]{2,1,0:T(8,128)S(1)} %copy-done.2, f32[1,512,512]{2,1,0:T(8,128)S(1)} %get-tuple-element.39, f32[1,512,512]{2,1,0:T(8,128)S(1)} %get-tuple-element.38), kind=kOutput, calls=%fused_computation.15 | convolution fusion | flops 1611005952 | bytes 6815744 | tf_op jit(solution)/shard_map/obr,osr->obs/dot_general | solution.py:283
  194.8 6.8 %convolution_convert_fusion = bf16[2,1024,384]{2,1,0:T(8,128)(2,1)S(1)} fusion(f32[2,1024,512]{2,1,0:T(8,128)S(1)} %copy-done.2, f32[1,512,512]{2,1,0:T(8,128)S(1)} %get-tuple-element.39, f32[1,512,512]{2,1,0:T(8,128)S(1)} %get-tuple-element.38), kind=kOutput, calls=%fused_computation.12 | convolution fusion | flops 4833017856 | bytes 7864320 | tf_op jit(solution)/shard_map/obr,osr->obs/dot_general | solution.py:286
  204.7 12.1 %collective-permute-done.30 = bf16[2,512,128]{2,1,0:T(8,128)(2,1)S(1)} collective-permute-done((bf16[2,512,128]{2,1,0:T(8,128)(2,1)S(1)}, bf16[2,512,128]{2,1,0:T(8,128)(2,1)S(1)}, u32[]{:S(2)}, u32[]{:S(2)}) %collective-permute-start.30) | collective-permute-done | bytes 262176 | tf_op jit(solution)/shard_map/ppermute | solution.py:182
  223.7 10.9 %collective-permute-done.35 = bf16[2,4,128,128]{3,2,1,0:T(8,128)(2,1)S(1)} collective-permute-done((bf16[2,4,128,128]{3,2,1,0:T(8,128)(2,1)S(1)}, bf16[2,4,128,128]{3,2,1,0:T(8,128)(2,1)S(1)}, u32[]{:S(2)}, u32[]{:S(2)}) %collective-permute-start.35) | collective-permute-done | bytes 262176 | tf_op jit(solution)/shard_map/ppermute | solution.py:182
  236.3 2.8 multiply_reduce_fusion.2
  242.7 2.5 collective-permute-start.38
  264.0 4.6 %collective-permute-done.46 = f32[4,32,512]{2,1,0:T(8,128)S(1)} collective-permute-done((f32[4,32,512]{2,1,0:T(8,128)S(1)}, f32[4,32,512]{2,1,0:T(8,128)S(1)}, u32[]{:S(2)}, u32[]{:S(2)}) %collective-permute-start.46) | collective-permute-done | bytes 262176 | tf_op jit(solution)/shard_map/ppermute | solution.py:182
  268.6 4.6 %collective-permute-done.45 = f32[4,32,512]{2,1,0:T(8,128)S(1)} collective-permute-done((f32[4,32,512]{2,1,0:T(8,128)S(1)}, f32[4,32,512]{2,1,0:T(8,128)S(1)}, u32[]{:S(2)}, u32[]{:S(2)}) %collective-permute-start.45) | collective-permute-done | bytes 262176 | tf_op jit(solution)/shard_map/ppermute | solution.py:182
  273.3 31.6 %inverse_factor.3 = f32[512,512]{1,0:T(8,128)S(1)} custom-call(s32[2]{0:T(128)S(1)} %pad_add_fusion.pos_ref, f32[4,4,32,512]{3,2,1,0:T(8,128)S(1)} %pad_maximum_fusion.4.pieces_ref), custom_call_target="tpu_custom_call" | custom-call | tf_op jit(solution)/shard_map/inverse_factor/pallas_call | solution.py:152
  305.2 2.5 collective-permute-done.47
  312.0 4.1 %fusion.4 = f32[2,256,512]{2,1,0:T(8,128)} fusion(f32[1,512,512]{2,1,0:T(8,128)S(1)} %get-tuple-element.37, f32[1,512,512]{2,1,0:T(8,128)S(1)} %get-tuple-element.36, f32[2,1024,512]{2,1,0:T(8,128)} %copy-done, s32[]{:T(128)S(6)} %select_n.459), kind=kOutput, calls=%fused_computation.8 | convolution fusion | flops 1611137024 | bytes 4194308 | tf_op jit(solution)/shard_map/obr,osr->obs/dot_general | solution.py:291
  (223 shorter events, 106.0 us)
Async XLA Ops:
  7.2 101.9 %all-gather.2.cloned.1.call-start = ((), (), s32[]{:S(2)}) async-start(), calls=%async_computation.1 | async-start | bytes 2621440 | tf_op jit(solution)/shard_map/all_gather | solution.py:224
  8.6 40.2 %collective-permute-start = (bf16[128,2048]{0,1:T(8,128)(2,1)S(1)}, bf16[128,2048]{0,1:T(8,128)(2,1)S(1)}, u32[]{:S(2)}, u32[]{:S(2)}) collective-permute-start(bf16[128,2048]{0,1:T(8,128)(2,1)S(1)} %copy.30), channel_id=1, source_target_pairs={{0,8},{8,0},{16,24},{24,16},{1,9},{9,1},{17,25},{25,17},{2,10},{10... | collective-permute-start | bytes 1572872 | tf_op jit(solution)/shard_map/ppermute | solution.py:182
  11.6 37.2 %collective-permute-start.1 = (bf16[128,2048]{0,1:T(8,128)(2,1)S(1)}, bf16[128,2048]{0,1:T(8,128)(2,1)S(1)}, u32[]{:S(2)}, u32[]{:S(2)}) collective-permute-start(bf16[128,2048]{0,1:T(8,128)(2,1)S(1)} %copy.30), channel_id=1, source_target_pairs={{0,16},{8,24},{16,0},{24,8},{1,17},{9,25},{17,1},{25,9},{2,18},{10... | collective-permute-start | bytes 1572872 | tf_op jit(solution)/shard_map/ppermute | solution.py:182
  13.1 35.7 %collective-permute-start.2 = (bf16[128,2048]{0,1:T(8,128)(2,1)S(1)}, bf16[128,2048]{0,1:T(8,128)(2,1)S(1)}, u32[]{:S(2)}, u32[]{:S(2)}) collective-permute-start(bf16[128,2048]{0,1:T(8,128)(2,1)S(1)} %copy.30), channel_id=1, source_target_pairs={{0,24},{8,16},{16,8},{24,0},{1,25},{9,17},{17,9},{25,1},{2,26},{10... | collective-permute-start | bytes 1572872 | tf_op jit(solution)/shard_map/ppermute | solution.py:182
  14.5 27.4 %collective-permute-start.4 = (bf16[2,256,128]{2,1,0:T(8,128)(2,1)S(1)}, bf16[2,256,128]{2,1,0:T(8,128)(2,1)}, u32[]{:S(2)}, u32[]{:S(2)}) collective-permute-start(bf16[2,256,128]{2,1,0:T(8,128)(2,1)S(1)} %get-tuple-element.50), channel_id=1, source_target_pairs={{0,16},{8,24},{16,0},{24,8},{1,17},{9,25},{17,1},{25,9},{2,18},{10... | collective-permute-start | bytes 393224 | tf_op jit(solution)/shard_map/ppermute | solution.py:182
  16.6 28.0 %collective-permute-start.5 = (bf16[2,256,128]{2,1,0:T(8,128)(2,1)S(1)}, bf16[2,256,128]{2,1,0:T(8,128)(2,1)}, u32[]{:S(2)}, u32[]{:S(2)}) collective-permute-start(bf16[2,256,128]{2,1,0:T(8,128)(2,1)S(1)} %get-tuple-element.49), channel_id=1, source_target_pairs={{0,24},{8,16},{16,8},{24,0},{1,25},{9,17},{17,9},{25,1},{2,26},{10... | collective-permute-start | bytes 393224 | tf_op jit(solution)/shard_map/ppermute | solution.py:182
  58.9 20.0 %collective-permute-start.9 = (bf16[2,512,128]{2,1,0:T(8,128)(2,1)}, bf16[2,512,128]{2,1,0:T(8,128)(2,1)}, u32[]{:S(2)}, u32[]{:S(2)}) collective-permute-start(bf16[2,512,128]{2,1,0:T(8,128)(2,1)} %convolution_convert_fusion.3), channel_id=1, source_target_pairs={{0,2},{1,3},{2,0},{3,1},{4,6},{5,7},{6,4},{7,5},{8,10},{9,11},{10,... | collective-permute-start | bytes 786440 | tf_op jit(solution)/shard_map/ppermute | solution.py:182
  58.9 20.9 %collective-permute-start.7 = (bf16[2,512,128]{2,1,0:T(8,128)(2,1)}, bf16[2,512,128]{2,1,0:T(8,128)(2,1)}, u32[]{:S(2)}, u32[]{:S(2)}) collective-permute-start(bf16[2,512,128]{2,1,0:T(8,128)(2,1)} %convolution_convert_fusion.3), channel_id=1, source_target_pairs={{0,1},{1,0},{2,3},{3,2},{4,5},{5,4},{6,7},{7,6},{8,9},{9,8},{10,11... | collective-permute-start | bytes 786440 | tf_op jit(solution)/shard_map/ppermute | solution.py:182
  59.7 21.8 %collective-permute-start.6 = (bf16[2,512,128]{2,1,0:T(8,128)(2,1)}, bf16[2,512,128]{2,1,0:T(8,128)(2,1)}, u32[]{:S(2)}, u32[]{:S(2)}) collective-permute-start(bf16[2,512,128]{2,1,0:T(8,128)(2,1)} %convolution_convert_fusion.3), channel_id=1, source_target_pairs={{0,4},{4,0},{1,5},{5,1},{2,6},{6,2},{3,7},{7,3},{8,12},{12,8},{9,1... | collective-permute-start | bytes 786440 | tf_op jit(solution)/shard_map/ppermute | solution.py:182
  61.5 243.7 %reduce-scatter.4.cloned.1.call-start = ((), (), s32[]{:S(2)}) async-start(), calls=%async_computation.2 | async-start | bytes 589824
  66.4 16.1 %collective-permute-start.12 = (bf16[2,512,128]{2,1,0:T(8,128)(2,1)}, bf16[2,512,128]{2,1,0:T(8,128)(2,1)S(1)}, u32[]{:S(2)}, u32[]{:S(2)}) collective-permute-start(bf16[2,512,128]{2,1,0:T(8,128)(2,1)} %collective-permute-done.11), channel_id=1, source_target_pairs={{0,4},{4,0},{1,5},{5,1},{2,6},{6,2},{3,7},{7,3},{8,12},{12,8},{9,1... | collective-permute-start | bytes 786440 | tf_op jit(solution)/shard_map/ppermute | solution.py:182
  83.5 21.0 %collective-permute-start.15 = (bf16[2,4,128,128]{3,2,1,0:T(8,128)(2,1)S(1)}, bf16[2,4,128,128]{3,2,1,0:T(8,128)(2,1)S(1)}, u32[]{:S(2)}, u32[]{:S(2)}) collective-permute-start(bf16[2,4,128,128]{3,2,1,0:T(8,128)(2,1)S(1)} %add_convert_fusion.2), channel_id=1, source_target_pairs={{0,24},{8,16},{16,8},{24,0},{1,25},{9,17},{17,9},{25,1},{2,26},{10... | collective-permute-start | bytes 786440 | tf_op jit(solution)/shard_map/ppermute | solution.py:182
  85.1 19.4 %collective-permute-start.14 = (bf16[2,4,128,128]{3,2,1,0:T(8,128)(2,1)S(1)}, bf16[2,4,128,128]{3,2,1,0:T(8,128)(2,1)S(1)}, u32[]{:S(2)}, u32[]{:S(2)}) collective-permute-start(bf16[2,4,128,128]{3,2,1,0:T(8,128)(2,1)S(1)} %add_convert_fusion.2), channel_id=1, source_target_pairs={{0,16},{8,24},{16,0},{24,8},{1,17},{9,25},{17,1},{25,9},{2,18},{10... | collective-permute-start | bytes 786440 | tf_op jit(solution)/shard_map/ppermute | solution.py:182
  85.6 22.7 %collective-permute-start.13 = (bf16[2,4,128,128]{3,2,1,0:T(8,128)(2,1)S(1)}, bf16[2,4,128,128]{3,2,1,0:T(8,128)(2,1)S(1)}, u32[]{:S(2)}, u32[]{:S(2)}) collective-permute-start(bf16[2,4,128,128]{3,2,1,0:T(8,128)(2,1)S(1)} %add_convert_fusion.2), channel_id=1, source_target_pairs={{0,8},{8,0},{16,24},{24,16},{1,9},{9,1},{17,25},{25,17},{2,10},{10... | collective-permute-start | bytes 786440 | tf_op jit(solution)/shard_map/ppermute | solution.py:182
  138.6 13.0 %collective-permute-start.24 = (f32[4,32,512]{2,1,0:T(8,128)S(1)}, f32[4,32,512]{2,1,0:T(8,128)S(1)}, u32[]{:S(2)}, u32[]{:S(2)}) collective-permute-start(f32[4,32,512]{2,1,0:T(8,128)S(1)} %get-tuple-element.99), channel_id=1, source_target_pairs={{0,16},{8,24},{16,0},{24,8},{1,17},{9,25},{17,1},{25,9},{2,18},{10... | collective-permute-start | bytes 786440 | tf_op jit(solution)/shard_map/ppermute | solution.py:182
  201.5 15.4 %collective-permute-start.30 = (bf16[2,512,128]{2,1,0:T(8,128)(2,1)S(1)}, bf16[2,512,128]{2,1,0:T(8,128)(2,1)S(1)}, u32[]{:S(2)}, u32[]{:S(2)}) collective-permute-start(bf16[2,512,128]{2,1,0:T(8,128)(2,1)S(1)} %convolution_convert_fusion.2), channel_id=1, source_target_pairs={{0,2},{1,3},{2,0},{3,1},{4,6},{5,7},{6,4},{7,5},{8,10},{9,11},{10,... | collective-permute-start | bytes 786440 | tf_op jit(solution)/shard_map/ppermute | solution.py:182
  201.6 15.4 %collective-permute-start.28 = (bf16[2,512,128]{2,1,0:T(8,128)(2,1)S(1)}, bf16[2,512,128]{2,1,0:T(8,128)(2,1)S(1)}, u32[]{:S(2)}, u32[]{:S(2)}) collective-permute-start(bf16[2,512,128]{2,1,0:T(8,128)(2,1)S(1)} %convolution_convert_fusion.2), channel_id=1, source_target_pairs={{0,1},{1,0},{2,3},{3,2},{4,5},{5,4},{6,7},{7,6},{8,9},{9,8},{10,11... | collective-permute-start | bytes 786440 | tf_op jit(solution)/shard_map/ppermute | solution.py:182
  204.0 13.6 %collective-permute-start.27 = (bf16[2,512,128]{2,1,0:T(8,128)(2,1)S(1)}, bf16[2,512,128]{2,1,0:T(8,128)(2,1)S(1)}, u32[]{:S(2)}, u32[]{:S(2)}) collective-permute-start(bf16[2,512,128]{2,1,0:T(8,128)(2,1)S(1)} %convolution_convert_fusion.2), channel_id=1, source_target_pairs={{0,4},{4,0},{1,5},{5,1},{2,6},{6,2},{3,7},{7,3},{8,12},{12,8},{9,1... | collective-permute-start | bytes 786440 | tf_op jit(solution)/shard_map/ppermute | solution.py:182
  204.1 13.6 %collective-permute-start.33 = (bf16[2,512,128]{2,1,0:T(8,128)(2,1)S(1)}, bf16[2,512,128]{2,1,0:T(8,128)(2,1)S(1)}, u32[]{:S(2)}, u32[]{:S(2)}) collective-permute-start(bf16[2,512,128]{2,1,0:T(8,128)(2,1)S(1)} %collective-permute-done.32), channel_id=1, source_target_pairs={{0,4},{4,0},{1,5},{5,1},{2,6},{6,2},{3,7},{7,3},{8,12},{12,8},{9,1... | collective-permute-start | bytes 786440 | tf_op jit(solution)/shard_map/ppermute | solution.py:182
  219.5 15.1 %collective-permute-start.36 = (bf16[2,4,128,128]{3,2,1,0:T(8,128)(2,1)S(1)}, bf16[2,4,128,128]{3,2,1,0:T(8,128)(2,1)S(1)}, u32[]{:S(2)}, u32[]{:S(2)}) collective-permute-start(bf16[2,4,128,128]{3,2,1,0:T(8,128)(2,1)S(1)} %add_convert_fusion), channel_id=1, source_target_pairs={{0,24},{8,16},{16,8},{24,0},{1,25},{9,17},{17,9},{25,1},{2,26},{10... | collective-permute-start | bytes 786440 | tf_op jit(solution)/shard_map/ppermute | solution.py:182
  220.9 13.7 %collective-permute-start.35 = (bf16[2,4,128,128]{3,2,1,0:T(8,128)(2,1)S(1)}, bf16[2,4,128,128]{3,2,1,0:T(8,128)(2,1)S(1)}, u32[]{:S(2)}, u32[]{:S(2)}) collective-permute-start(bf16[2,4,128,128]{3,2,1,0:T(8,128)(2,1)S(1)} %add_convert_fusion), channel_id=1, source_target_pairs={{0,16},{8,24},{16,0},{24,8},{1,17},{9,25},{17,1},{25,9},{2,18},{10... | collective-permute-start | bytes 786440 | tf_op jit(solution)/shard_map/ppermute | solution.py:182
  222.0 12.8 %collective-permute-start.34 = (bf16[2,4,128,128]{3,2,1,0:T(8,128)(2,1)S(1)}, bf16[2,4,128,128]{3,2,1,0:T(8,128)(2,1)S(1)}, u32[]{:S(2)}, u32[]{:S(2)}) collective-permute-start(bf16[2,4,128,128]{3,2,1,0:T(8,128)(2,1)S(1)} %add_convert_fusion), channel_id=1, source_target_pairs={{0,8},{8,0},{16,24},{24,16},{1,9},{9,1},{17,25},{25,17},{2,10},{10... | collective-permute-start | bytes 786440 | tf_op jit(solution)/shard_map/ppermute | solution.py:182
  259.8 13.5 %collective-permute-start.45 = (f32[4,32,512]{2,1,0:T(8,128)S(1)}, f32[4,32,512]{2,1,0:T(8,128)S(1)}, u32[]{:S(2)}, u32[]{:S(2)}) collective-permute-start(f32[4,32,512]{2,1,0:T(8,128)S(1)} %get-tuple-element.52), channel_id=1, source_target_pairs={{0,16},{8,24},{16,0},{24,8},{1,17},{9,25},{17,1},{25,9},{2,18},{10... | collective-permute-start | bytes 786440 | tf_op jit(solution)/shard_map/ppermute | solution.py:182
  260.9 12.4 %collective-permute-start.44 = (f32[4,32,512]{2,1,0:T(8,128)S(1)}, f32[4,32,512]{2,1,0:T(8,128)S(1)}, u32[]{:S(2)}, u32[]{:S(2)}) collective-permute-start(f32[4,32,512]{2,1,0:T(8,128)S(1)} %get-tuple-element.52), channel_id=1, source_target_pairs={{0,8},{8,0},{16,24},{24,16},{1,9},{9,1},{17,25},{25,17},{2,10},{10... | collective-permute-start | bytes 786440 | tf_op jit(solution)/shard_map/ppermute | solution.py:182
  (56 other events, 617.6 us)
Sparse Core Ops, SparseCore 0:
  61.6 47.0 all-gather.1
  264.1 30.7 reduce-scatter.3

commit v4 on v3

--- a/solution.py
+++ b/solution.py
@@ -15,12 +15,25 @@
 
 ridge = 2.0
 HIGHEST = lax.Precision.HIGHEST
-
-
-def reciprocal(value):
-    guess = pl.reciprocal(value, approx=True)
-    guess = guess * (2.0 - value * guess)
-    return guess * (2.0 - value * guess)
+HIGH = lax.Precision.HIGH
+
+
+def split(value):
+    high = lax.reduce_precision(value, 8, 7)
+    return high.astype(jnp.bfloat16), (value - high).astype(jnp.bfloat16)
+
+
+def kernel_dot(left, right, exact):
+    if exact:
+        return jnp.dot(left, right, preferred_element_type=jnp.float32, precision=HIGHEST)
+    parts = []
+    for value in (left, right):
+        high = value.astype(jnp.bfloat16)
+        parts.append((high, (value - high.astype(jnp.float32)).astype(jnp.bfloat16)))
+    (a, b), (c, d) = parts
+    return sum(
+        jnp.dot(x, y, preferred_element_type=jnp.float32) for x, y in ((b, c), (a, d), (a, c))
+    )
 
 
 def eliminate(tiles, inv_ref):
@@ -46,7 +59,7 @@
         below = [[None] * SUB for _ in range(SUB)]
         inverse = []
         for b in range(SUB):
-            inverse.append(reciprocal(pivot[b][b]))
+            inverse.append(pl.reciprocal(pivot[b][b], approx=True))
             for i in range(b + 1, SUB):
                 factor = pivot[b][i] * inverse[b]
                 below[i][b] = factor
@@ -55,9 +68,7 @@
                 rows[i] = rows[i] - factor * rows[b]
         result = jnp.zeros(shape, jnp.float32)
         for b in range(SUB):
-            root = lax.rsqrt(pivot[b][b])
-            root = root * (1.5 - 0.5 * pivot[b][b] * root * root)
-            result = jnp.where(sub == b, rows[b] * root, result)
+            result = jnp.where(sub == b, rows[b] * lax.rsqrt(pivot[b][b]), result)
         inv_ref[start : start + SUB, :] = jnp.where(lane < start + SUB, result, 0.0)
         solved = [None] * SUB
         for b in reversed(range(SUB)):
@@ -74,7 +85,7 @@
             tiles[q] = jnp.where(inside, 0.0, tiles[q]) - parts[0]
 
 
-def factor_kernel(scale, own_cols, rows_moved, pos_ref, pieces_ref, out_ref, work_ref, inv_ref):
+def factor_kernel(scale, own_cols, rows_moved, exact, pos_ref, pieces_ref, out_ref, work_ref, inv_ref):
     tok_count, gc_count, rows, rank = pieces_ref.shape
     panels = rank // PANEL
     tok_pos, gc_pos = pos_ref[0], pos_ref[1]
@@ -88,25 +99,19 @@
         diag = work_ref[here, here]
 
         eliminate([diag[SUB * q : SUB * (q + 1), :] for q in range(PANEL // SUB)], inv_ref)
-        inv = inv_ref[...]
-        work_ref[here, :] = jnp.dot(
-            inv, work_ref[here, :], preferred_element_type=jnp.float32, precision=HIGHEST
-        )
-        work_ref[here, here] = inv
-        for i in range(1, panels):
-
-            @pl.when(i > k)
+        for here_k in range(panels):
+
+            @pl.when(k == here_k)
             def _():
-                below = pl.ds(i * PANEL, PANEL)
-                work_ref[below, here] = jnp.zeros((PANEL, PANEL), jnp.float32)
-                upper = work_ref[here, :]
-                work_ref[below, :] -= lax.dot_general(
-                    upper[:, i * PANEL : (i + 1) * PANEL],
-                    upper,
-                    (((0,), (0,)), ((), ())),
-                    preferred_element_type=jnp.float32,
-                    precision=HIGHEST,
-                )
+                panel = slice(here_k * PANEL, (here_k + 1) * PANEL)
+                rest = slice((here_k + 1) * PANEL, rank)
+                inv = inv_ref[...]
+                work_ref[panel, :] = kernel_dot(inv, work_ref[panel, :], exact)
+                work_ref[panel, panel] = inv
+                if here_k < panels - 1:
+                    lower = work_ref[panel, rest].T
+                    work_ref[rest, panel] = jnp.zeros((rank - rest.start, PANEL), jnp.float32)
+                    work_ref[rest, :] -= kernel_dot(lower, work_ref[panel, :], exact)
 
         return carry
 
@@ -130,7 +135,7 @@
                 )
 
 
-def inverse_factor(pieces, own_cols, rows_moved, scale):
+def inverse_factor(pieces, own_cols, rows_moved, exact, scale):
     tok_count, gc_count, rows, rank = pieces.shape
     tok_pos, gc_pos = lax.axis_index("tok"), lax.axis_index("gc")
     aligned = own_cols % PANEL == 0 and rows % SUB == 0
@@ -150,7 +155,7 @@
         full = jnp.zeros((rank, rank), jnp.float32).at[place].set(pieces.reshape(rank, rank))
         pieces = full.reshape(1, 1, rank, rank)
     inverse = pl.pallas_call(
-        functools.partial(factor_kernel, scale, own_cols if aligned else rank, rows_moved),
+        functools.partial(factor_kernel, scale, own_cols if aligned else rank, rows_moved, exact),
         out_shape=jax.ShapeDtypeStruct((rank, rank), jnp.float32),
         in_specs=[
             pl.BlockSpec(memory_space=pltpu.SMEM),
@@ -171,11 +176,6 @@
     return inverse
 
 
-def split(value):
-    high = lax.reduce_precision(value, 8, 7)
-    return high.astype(jnp.bfloat16), (value - high).astype(jnp.bfloat16)
-
-
 def swap(value, axis, k):
     if k == 0:
         return value
@@ -184,6 +184,15 @@
 
 def collect(value, axis):
     return [swap(value, axis, k) for k in range(lax.axis_size(axis))]
+
+
+def collect_relayed(value, axis):
+    if lax.axis_size(axis) != 4:
+        return collect(value, axis)
+    half = value.shape[0] // 2
+    near, side = swap(value, axis, 1), swap(value, axis, 2)
+    far = [swap(side[:half], axis, 1), swap(near[half:], axis, 2)]
+    return [value, near, side, jnp.concatenate(far, axis=0)]
 
 
 def per_device(acts, init_basis, kept, member):
@@ -218,19 +227,30 @@
     own_basis = jnp.concatenate(
         [lax.select_n(tok_pos ^ a, *slices) for a in range(tok_count)], axis=1
     )
-    acts_pieces = collect(acts, "tok")
-    acts_pieces, init_late = lax.optimization_barrier((acts_pieces, init_bf))
+    acts_pieces = collect_relayed(acts, "tok")
+    early = 3 * len(acts_pieces) // 4
+    acts_pieces[-1], init_late = lax.optimization_barrier((acts_pieces[-1], init_bf))
+    chunks = [
+        jnp.concatenate(part, axis=0).reshape(-1, owned, block_cols)
+        for part in (acts_pieces[:early], acts_pieces[early:])
+    ]
     full_x = jnp.concatenate(acts_pieces, axis=0).reshape(total_tokens, owned, block_cols)
-    basis_bf = lax.all_gather(init_late, "tok", axis=1, tiled=True)
+    init_pieces = collect(init_late, "tok")
+    basis_bf = jnp.concatenate(
+        [lax.select_n(tok_pos ^ a, *init_pieces) for a in range(tok_count)], axis=1
+    )
     basis_bf = jnp.concatenate([columns_of(basis_bf, k) for k in range(tok_count)], axis=2)
 
-    def mix(own_basis):
+    def mix(x, own_basis):
         proj = jnp.einsum(
-            "tob,obr->otr", full_x, own_basis, preferred_element_type=jnp.float32
+            "tob,obr->otr", x, own_basis, preferred_element_type=jnp.float32
         ).astype(jnp.bfloat16)
         total = jnp.zeros(proj.shape, jnp.float32)
-        for b, near in enumerate(collect(proj, "gc")):
-            for a, piece in enumerate(collect(near, "gr")):
+        near = collect(proj, "gc")
+        across = swap(jnp.stack(near), "gr", 1)
+        for a in range(gr_count):
+            for b in range(gc_count):
+                piece = across[b] if a else near[b]
                 source = ((gr_pos ^ a) * gc_count + (gc_pos ^ b)) * owned
                 weights = lax.dynamic_slice_in_dim(own_links, source, owned, 1)
                 for j in range(owned):
@@ -246,8 +266,9 @@
             )
         return jnp.concatenate(pieces, axis=3).reshape(owned, total_tokens, rank)
 
-    def factor(image, rows_moved):
-        grams = jnp.einsum("obr,obs->ors", image[:, :, :own_cols], image, precision=HIGHEST)
+    def factor(image, last):
+        precision = HIGHEST if last else HIGH
+        grams = jnp.einsum("obr,obs->ors", image[:, :, :own_cols], image, precision=precision)
 
         def group_sum(g):
             mask = (own_groups == g).astype(jnp.float32)
@@ -266,7 +287,7 @@
         )
         near = jnp.stack(collect(piece, "gc"))
         pieces = jnp.stack(collect(near, "tok"))
-        own = inverse_factor(pieces, own_cols, rows_moved, 1.0 / group_cols)
+        own = inverse_factor(pieces, own_cols, not last, last, 1.0 / group_cols)
         other = swap(own, "gr", 1)
         of_block = jnp.stack(
             [jnp.where(own_groups[o] == gr_pos, own, other) for o in range(owned)]
@@ -275,20 +296,24 @@
         return of_block, of_group
 
     for step in range(ITERS):
-        mixed = gather_mixed(mix(own_basis))
+        if step == 0:
+            mixed = jnp.concatenate([mix(x, own_basis) for x in chunks], axis=1)
+        else:
+            mixed = mix(full_x, own_basis)
+        mixed = gather_mixed(mixed)
         cover = jnp.einsum("tob,otr->obr", full_x, mixed, preferred_element_type=jnp.float32)
         image = cover / total_tokens + ridge * basis_bf.astype(jnp.float32)
-        of_block, of_group = factor(image, step < ITERS - 1)
+        of_block, of_group = factor(image, step == ITERS - 1)
         if step < ITERS - 1:
             own_basis = jnp.einsum(
-                "obr,osr->obs", image, of_block[:, :own_cols], precision=HIGHEST
+                "obr,osr->obs", image, of_block[:, :own_cols], precision=HIGH
             ).astype(jnp.bfloat16)
             other_basis = jnp.einsum(
-                "obr,osr->obs", image, of_block[:, own_cols:], precision=HIGHEST
+                "obr,osr->obs", image, of_block[:, own_cols:], precision=HIGH
             ).astype(jnp.bfloat16)
             basis_bf = jnp.concatenate([own_basis, other_basis], axis=2)
     rows = lax.dynamic_slice_in_dim(image, tok_pos * slice_rows, slice_rows, 1)
-    basis = jnp.einsum("obr,osr->obs", rows, of_block, precision=HIGHEST)
+    basis = jnp.einsum("obr,osr->obs", rows, of_block, precision=HIGH)
     own_x = acts.reshape(tok_rows, owned, block_cols)
     codes = sum(
         jnp.einsum("tob,obr->otr", own_x, part, preferred_element_type=jnp.float32)
@@ -308,7 +333,7 @@
                 "tr,sr->ts",
                 placed[:, g * rank : (g + 1) * rank],
                 of_group[g],
-                precision=HIGHEST,
+                precision=HIGH,
             )
             for g in range(groups)
         ],

time: 329 us -> 295 us (0.90)
  Pallas kernels: 63.5 us -> 44.2 us
  other arithmetic: 19.3 us -> 9.43 us
  matrix products: 31.2 us -> 22.6 us
  local copies, waits for them, and re-layouts: 15 us -> 6.69 us
  starting transfers between devices: 51.8 us -> 60.1 us
  waiting for transfers between devices: 126 us -> 130 us
    pallas_call x2, Pallas kernels: 63.5 us -> 44.2 us  [inverse_factor(): pl.pallas_call(functools.partial(factor_kernel, scale, own_cols if aligne...]
    ppermute x48 -> x50, starting transfers between devices: 51.7 us -> 60.1 us  [swap(): lax.ppermute(value, axis, [(i, i ^ k) for i in range(lax.axis_size(axis))])]
    dot_general x7 -> x8, matrix products: 22.7 us -> 14.9 us  [the longest x2 4.18 us: factor(): jnp.einsum('obr,obs->ors', image[:, :, :own_cols], image, precision=preci...]
    mul x16 -> x12, other arithmetic: 6.66 us -> 0.45 us  [mix(): total += weights[:, j][:, None, None] * piece[j][None].astype(jnp.float32)]
    ppermute x48 -> x50, waiting for transfers between devices: 126 us -> 130 us  [swap(): lax.ppermute(value, axis, [(i, i ^ k) for i in range(lax.axis_size(axis))])]
    unnamed x62 -> x22, local copies, waits for them, and re-layouts: 7.98 us -> 4.33 us
  transfers between devices with their start and end apart: 50 -> 51, of which waited for: 28 -> 29; matrix products, arithmetic and copies ran while one was open for 9% -> 5% of each run, Pallas kernels for 10% -> 8%
where the time goes in v4:
time: 295 us; the launch traced here: 290 us
  waiting for transfers between devices  130 us (44%)
  starting transfers between devices  60.1 us (20%)
  Pallas kernels  44.2 us (15%)
  matrix products  22.6 us (8%)
  between operations  16.6 us (6%)
  other arithmetic  9.43 us (3%)
  local copies, waits for them, and re-layouts  6.69 us (2%)
    ppermute x50, waiting for transfers between devices, swap(): lax.ppermute(value, axis, [(i, i ^ k) for i in range(lax.axis_size(axis))])  130 us
    ppermute x50, starting transfers between devices, swap(): lax.ppermute(value, axis, [(i, i ^ k) for i in range(lax.axis_size(axis))])  60.1 us
    pallas_call x2, Pallas kernels, inverse_factor(): pl.pallas_call(functools.partial(factor_kernel, scale, own_cols if aligne...  44.2 us
  transfers between devices with their start and end apart: 51, of which 29 were waited for; matrix products, arithmetic and copies ran while one was open for 5% of the time, Pallas kernels for 8%

profile of v4, /device:TPU:0, one launch (start us, length us, event | category | flops | bytes accessed | tf_op | source)
XLA Modules:
  0.0 289.6 jit_solution(17577973541170246794)
XLA Ops:
  8.5 3.0 %collective-permute-start = (bf16[128,2048]{0,1:T(8,128)(2,1)S(1)}, bf16[128,2048]{0,1:T(8,128)(2,1)S(1)}, u32[]{:S(2)}, u32[]{:S(2)}) collective-permute-start(bf16[128,2048]{0,1:T(8,128)(2,1)S(1)} %copy.34), channel_id=1, source_target_pairs={{0,8},{8,0},{16,24},{24,16},{1,9},{9,1},{17,25},{25,17},{2,10},{10... | collective-permute-start | bytes 1572872 | tf_op jit(solution)/shard_map/ppermute | solution.py:182
  19.2 11.4 %collective-permute-done.5 = bf16[2,256,128]{2,1,0:T(8,128)(2,1)S(1)} collective-permute-done((bf16[2,256,128]{2,1,0:T(8,128)(2,1)S(1)}, bf16[2,256,128]{2,1,0:T(8,128)(2,1)S(1)}, u32[]{:S(2)}, u32[]{:S(2)}) %collective-permute-start.5) | collective-permute-done | bytes 131104 | tf_op jit(solution)/shard_map/ppermute | solution.py:182
  31.8 3.7 %collective-permute-start.9 = (bf16[2,384,128]{2,1,0:T(8,128)(2,1)S(1)}, bf16[2,384,128]{2,1,0:T(8,128)(2,1)S(1)}, u32[]{:S(2)}, u32[]{:S(2)}) collective-permute-start(bf16[2,384,128]{2,1,0:T(8,128)(2,1)S(1)} %convolution_convert_fusion.3), channel_id=1, source_target_pairs={{0,3},{1,2},{2,1},{3,0},{4,7},{5,6},{6,5},{7,4},{8,11},{9,10},{10,... | collective-permute-start | bytes 589832 | tf_op jit(solution)/shard_map/ppermute | solution.py:182
  38.6 2.9 collective-permute-done.9
  41.5 9.5 %collective-permute-done.8 = bf16[2,384,128]{2,1,0:T(8,128)(2,1)S(1)} collective-permute-done((bf16[2,384,128]{2,1,0:T(8,128)(2,1)S(1)}, bf16[2,384,128]{2,1,0:T(8,128)(2,1)S(1)}, u32[]{:S(2)}, u32[]{:S(2)}) %collective-permute-start.8) | collective-permute-done | bytes 196640 | tf_op jit(solution)/shard_map/ppermute | solution.py:182
  51.9 2.5 collective-permute-start.13
  63.6 17.4 %collective-permute-done.19 = bf16[2,256,512]{2,1,0:T(8,128)(2,1)S(1)} collective-permute-done((bf16[2,256,512]{2,1,0:T(8,128)(2,1)S(1)}, bf16[2,256,512]{2,1,0:T(8,128)(2,1)S(1)}, u32[]{:S(2)}, u32[]{:S(2)}) %collective-permute-start.19) | collective-permute-done | bytes 524320 | tf_op jit(solution)/shard_map/ppermute | solution.py:182
  81.1 3.0 %collective-permute-done.18 = bf16[2,256,512]{2,1,0:T(8,128)(2,1)S(1)} collective-permute-done((bf16[2,256,512]{2,1,0:T(8,128)(2,1)S(1)}, bf16[2,256,512]{2,1,0:T(8,128)(2,1)S(1)}, u32[]{:S(2)}, u32[]{:S(2)}) %collective-permute-start.18) | collective-permute-done | bytes 524320 | tf_op jit(solution)/shard_map/ppermute | solution.py:182
  89.2 8.1 %collective-permute-done.16 = bf16[2,4,128,128]{3,2,1,0:T(8,128)(2,1)S(1)} collective-permute-done((bf16[2,4,128,128]{3,2,1,0:T(8,128)(2,1)S(1)}, bf16[2,4,128,128]{3,2,1,0:T(8,128)(2,1)S(1)}, u32[]{:S(2)}, u32[]{:S(2)}) %collective-permute-start.16) | collective-permute-done | bytes 262176 | tf_op jit(solution)/shard_map/ppermute | solution.py:182
  126.9 6.5 %collective-permute-done.30 = f32[4,32,512]{2,1,0:T(8,128)S(1)} collective-permute-done((f32[4,32,512]{2,1,0:T(8,128)S(1)}, f32[4,32,512]{2,1,0:T(8,128)S(1)}, u32[]{:S(2)}, u32[]{:S(2)}) %collective-permute-start.30) | collective-permute-done | bytes 262176 | tf_op jit(solution)/shard_map/ppermute | solution.py:182
  133.4 4.0 %collective-permute-done.29 = f32[4,32,512]{2,1,0:T(8,128)S(1)} collective-permute-done((f32[4,32,512]{2,1,0:T(8,128)S(1)}, f32[4,32,512]{2,1,0:T(8,128)S(1)}, u32[]{:S(2)}, u32[]{:S(2)}) %collective-permute-start.29) | collective-permute-done | bytes 262176 | tf_op jit(solution)/shard_map/ppermute | solution.py:182
  137.5 21.6 %inverse_factor.2 = f32[512,512]{1,0:T(8,128)S(1)} custom-call(s32[2]{0:T(128)S(1)} %pad_add_fusion.pos_ref, f32[4,4,32,512]{3,2,1,0:T(8,128)S(1)} %pad_maximum_fusion.5.pieces_ref), custom_call_target="tpu_custom_call" | custom-call | tf_op jit(solution)/shard_map/inverse_factor/pallas_call | solution.py:157
  171.2 6.6 %collective-permute-done.34 = bf16[2,512,128]{2,1,0:T(8,128)(2,1)S(1)} collective-permute-done((bf16[2,512,128]{2,1,0:T(8,128)(2,1)S(1)}, bf16[2,512,128]{2,1,0:T(8,128)(2,1)S(1)}, u32[]{:S(2)}, u32[]{:S(2)}) %collective-permute-start.34) | collective-permute-done | bytes 262176 | tf_op jit(solution)/shard_map/ppermute | solution.py:182
  177.8 13.3 %collective-permute-done.33 = bf16[2,512,128]{2,1,0:T(8,128)(2,1)S(1)} collective-permute-done((bf16[2,512,128]{2,1,0:T(8,128)(2,1)S(1)}, bf16[2,512,128]{2,1,0:T(8,128)(2,1)S(1)}, u32[]{:S(2)}, u32[]{:S(2)}) %collective-permute-start.33) | collective-permute-done | bytes 262176 | tf_op jit(solution)/shard_map/ppermute | solution.py:182
  191.3 3.5 %convolution_convert_fusion = bf16[2,1024,384]{2,1,0:T(8,128)(2,1)S(1)} fusion(f32[2,1024,512]{2,1,0:T(8,128)S(1)} %copy-done.2, f32[1,512,512]{2,1,0:T(8,128)S(1)} %get-tuple-element.33, f32[1,512,512]{2,1,0:T(8,128)S(1)} %get-tuple-element.32), kind=kOutput, calls=%fused_computation.13 | convolution fusion | flops 2417098752 | bytes 7864320 | tf_op jit(solution)/shard_map/obr,osr->obs/dot_general | solution.py:311
  200.3 11.1 %collective-permute-done.37 = bf16[2,4,128,128]{3,2,1,0:T(8,128)(2,1)S(1)} collective-permute-done((bf16[2,4,128,128]{3,2,1,0:T(8,128)(2,1)S(1)}, bf16[2,4,128,128]{3,2,1,0:T(8,128)(2,1)S(1)}, u32[]{:S(2)}, u32[]{:S(2)}) %collective-permute-start.37) | collective-permute-done | bytes 262176 | tf_op jit(solution)/shard_map/ppermute | solution.py:182
  213.4 2.6 multiply_reduce_fusion.2
  219.6 2.6 collective-permute-start.40
  228.5 2.6 collective-permute-start.43
  240.8 4.7 %collective-permute-done.48 = f32[4,32,512]{2,1,0:T(8,128)S(1)} collective-permute-done((f32[4,32,512]{2,1,0:T(8,128)S(1)}, f32[4,32,512]{2,1,0:T(8,128)S(1)}, u32[]{:S(2)}, u32[]{:S(2)}) %collective-permute-start.48) | collective-permute-done | bytes 262176 | tf_op jit(solution)/shard_map/ppermute | solution.py:182
  245.5 4.6 %collective-permute-done.47 = f32[4,32,512]{2,1,0:T(8,128)S(1)} collective-permute-done((f32[4,32,512]{2,1,0:T(8,128)S(1)}, f32[4,32,512]{2,1,0:T(8,128)S(1)}, u32[]{:S(2)}, u32[]{:S(2)}) %collective-permute-start.47) | collective-permute-done | bytes 262176 | tf_op jit(solution)/shard_map/ppermute | solution.py:182
  250.2 22.5 %inverse_factor.3 = f32[512,512]{1,0:T(8,128)S(1)} custom-call(s32[2]{0:T(128)S(1)} %pad_add_fusion.pos_ref, f32[4,4,32,512]{3,2,1,0:T(8,128)S(1)} %pad_maximum_fusion.7.pieces_ref), custom_call_target="tpu_custom_call" | custom-call | tf_op jit(solution)/shard_map/inverse_factor/pallas_call | solution.py:157
  272.9 2.5 collective-permute-done.49
  278.9 3.4 %fusion.4 = f32[2,256,512]{2,1,0:T(8,128)} fusion(f32[1,512,512]{2,1,0:T(8,128)S(1)} %get-tuple-element.31, f32[1,512,512]{2,1,0:T(8,128)S(1)} %get-tuple-element.30, f32[2,1024,512]{2,1,0:T(8,128)} %copy-done, s32[]{:T(128)S(6)} %select_n.575), kind=kOutput, calls=%fused_computation.9 | convolution fusion | flops 805830656 | bytes 4194308 | tf_op jit(solution)/shard_map/obr,osr->obs/dot_general | solution.py:316
  (192 shorter events, 99.4 us)
Async XLA Ops:
  7.2 265.7 %reduce-scatter.4.cloned.1.call-start = ((), (), s32[]{:S(2)}) async-start(), calls=%async_computation.1 | async-start | bytes 589824
  8.5 22.2 %collective-permute-start = (bf16[128,2048]{0,1:T(8,128)(2,1)S(1)}, bf16[128,2048]{0,1:T(8,128)(2,1)S(1)}, u32[]{:S(2)}, u32[]{:S(2)}) collective-permute-start(bf16[128,2048]{0,1:T(8,128)(2,1)S(1)} %copy.34), channel_id=1, source_target_pairs={{0,8},{8,0},{16,24},{24,16},{1,9},{9,1},{17,25},{25,17},{2,10},{10... | collective-permute-start | bytes 1572872 | tf_op jit(solution)/shard_map/ppermute | solution.py:182
  11.6 19.2 %collective-permute-start.1 = (bf16[128,2048]{0,1:T(8,128)(2,1)S(1)}, bf16[128,2048]{0,1:T(8,128)(2,1)S(1)}, u32[]{:S(2)}, u32[]{:S(2)}) collective-permute-start(bf16[128,2048]{0,1:T(8,128)(2,1)S(1)} %copy.34), channel_id=1, source_target_pairs={{0,16},{8,24},{16,0},{24,8},{1,17},{9,25},{17,1},{25,9},{2,18},{10... | collective-permute-start | bytes 1572872 | tf_op jit(solution)/shard_map/ppermute | solution.py:182
  14.5 16.1 %collective-permute-start.5 = (bf16[2,256,128]{2,1,0:T(8,128)(2,1)S(1)}, bf16[2,256,128]{2,1,0:T(8,128)(2,1)S(1)}, u32[]{:S(2)}, u32[]{:S(2)}) collective-permute-start(bf16[2,256,128]{2,1,0:T(8,128)(2,1)S(1)} %get-tuple-element.72), channel_id=1, source_target_pairs={{0,16},{8,24},{16,0},{24,8},{1,17},{9,25},{17,1},{25,9},{2,18},{10... | collective-permute-start | bytes 393224 | tf_op jit(solution)/shard_map/ppermute | solution.py:182
  15.0 15.5 %collective-permute-start.6 = (bf16[2,256,128]{2,1,0:T(8,128)(2,1)S(1)}, bf16[2,256,128]{2,1,0:T(8,128)(2,1)S(1)}, u32[]{:S(2)}, u32[]{:S(2)}) collective-permute-start(bf16[2,256,128]{2,1,0:T(8,128)(2,1)S(1)} %get-tuple-element.71), channel_id=1, source_target_pairs={{0,24},{8,16},{16,8},{24,0},{1,25},{9,17},{17,9},{25,1},{2,26},{10... | collective-permute-start | bytes 393224 | tf_op jit(solution)/shard_map/ppermute | solution.py:182
  16.5 14.0 %collective-permute-start.4 = (bf16[2,256,128]{2,1,0:T(8,128)(2,1)S(1)}, bf16[2,256,128]{2,1,0:T(8,128)(2,1)S(1)}, u32[]{:S(2)}, u32[]{:S(2)}) collective-permute-start(bf16[2,256,128]{2,1,0:T(8,128)(2,1)S(1)} %get-tuple-element.70), channel_id=1, source_target_pairs={{0,8},{8,0},{16,24},{24,16},{1,9},{9,1},{17,25},{25,17},{2,10},{10... | collective-permute-start | bytes 393224 | tf_op jit(solution)/shard_map/ppermute | solution.py:182
  35.4 15.5 %collective-permute-start.8 = (bf16[2,384,128]{2,1,0:T(8,128)(2,1)S(1)}, bf16[2,384,128]{2,1,0:T(8,128)(2,1)S(1)}, u32[]{:S(2)}, u32[]{:S(2)}) collective-permute-start(bf16[2,384,128]{2,1,0:T(8,128)(2,1)S(1)} %convolution_convert_fusion.3), channel_id=1, source_target_pairs={{0,2},{1,3},{2,0},{3,1},{4,6},{5,7},{6,4},{7,5},{8,10},{9,11},{10,... | collective-permute-start | bytes 589832 | tf_op jit(solution)/shard_map/ppermute | solution.py:182
  35.4 15.5 %collective-permute-start.7 = (bf16[2,384,128]{2,1,0:T(8,128)(2,1)S(1)}, bf16[2,384,128]{2,1,0:T(8,128)(2,1)S(1)}, u32[]{:S(2)}, u32[]{:S(2)}) collective-permute-start(bf16[2,384,128]{2,1,0:T(8,128)(2,1)S(1)} %convolution_convert_fusion.3), channel_id=1, source_target_pairs={{0,1},{1,0},{2,3},{3,2},{4,5},{5,4},{6,7},{7,6},{8,9},{9,8},{10,11... | collective-permute-start | bytes 589832 | tf_op jit(solution)/shard_map/ppermute | solution.py:182
  36.4 14.8 %collective-permute-start.3 = (bf16[64,2048]{0,1:T(8,128)(2,1)S(1)}, bf16[64,2048]{0,1:T(8,128)(2,1)S(1)}, u32[]{:S(2)}, u32[]{:S(2)}) collective-permute-start(bf16[64,2048]{0,1:T(8,128)(2,1)S(1)} %slice.521), channel_id=1, source_target_pairs={{0,16},{8,24},{16,0},{24,8},{1,17},{9,25},{17,1},{25,9},{2,18},{10... | collective-permute-start | bytes 786440 | tf_op jit(solution)/shard_map/ppermute | solution.py:182
  38.0 13.2 %collective-permute-start.2 = (bf16[64,2048]{0,1:T(8,128)(2,1)S(1)}, bf16[64,2048]{0,1:T(8,128)(2,1)S(1)}, u32[]{:S(2)}, u32[]{:S(2)}) collective-permute-start(bf16[64,2048]{0,1:T(8,128)(2,1)S(1)} %bitcast.291), channel_id=1, source_target_pairs={{0,8},{8,0},{16,24},{24,16},{1,9},{9,1},{17,25},{25,17},{2,10},{10... | collective-permute-start | bytes 786440 | tf_op jit(solution)/shard_map/ppermute | solution.py:182
  51.1 33.3 %collective-permute-start.10 = (bf16[4,2,384,128]{3,2,1,0:T(8,128)(2,1)S(1)}, bf16[4,2,384,128]{3,2,1,0:T(8,128)(2,1)S(1)}, u32[]{:S(2)}, u32[]{:S(2)}) collective-permute-start(bf16[4,2,384,128]{3,2,1,0:T(8,128)(2,1)S(1)} %pad_maximum_fusion.8), channel_id=1, source_target_pairs={{0,4},{4,0},{1,5},{5,1},{2,6},{6,2},{3,7},{7,3},{8,12},{12,8},{9,1... | collective-permute-start | bytes 2359304 | tf_op jit(solution)/shard_map/ppermute | solution.py:182
  56.4 24.7 %collective-permute-start.19 = (bf16[2,256,512]{2,1,0:T(8,128)(2,1)S(1)}, bf16[2,256,512]{2,1,0:T(8,128)(2,1)S(1)}, u32[]{:S(2)}, u32[]{:S(2)}) collective-permute-start(bf16[2,256,512]{2,1,0:T(8,128)(2,1)S(1)} %convert_element_type.416), channel_id=1, source_target_pairs={{0,16},{8,24},{16,0},{24,8},{1,17},{9,25},{17,1},{25,9},{2,18},{10... | collective-permute-start | bytes 1572872 | tf_op jit(solution)/shard_map/ppermute | solution.py:182
  58.7 22.4 %collective-permute-start.20 = (bf16[2,256,512]{2,1,0:T(8,128)(2,1)S(1)}, bf16[2,256,512]{2,1,0:T(8,128)(2,1)S(1)}, u32[]{:S(2)}, u32[]{:S(2)}) collective-permute-start(bf16[2,256,512]{2,1,0:T(8,128)(2,1)S(1)} %convert_element_type.416), channel_id=1, source_target_pairs={{0,24},{8,16},{16,8},{24,0},{1,25},{9,17},{17,9},{25,1},{2,26},{10... | collective-permute-start | bytes 1572872 | tf_op jit(solution)/shard_map/ppermute | solution.py:182
  61.1 23.0 %collective-permute-start.18 = (bf16[2,256,512]{2,1,0:T(8,128)(2,1)S(1)}, bf16[2,256,512]{2,1,0:T(8,128)(2,1)S(1)}, u32[]{:S(2)}, u32[]{:S(2)}) collective-permute-start(bf16[2,256,512]{2,1,0:T(8,128)(2,1)S(1)} %convert_element_type.416), channel_id=1, source_target_pairs={{0,8},{8,0},{16,24},{24,16},{1,9},{9,1},{17,25},{25,17},{2,10},{10... | collective-permute-start | bytes 1572872 | tf_op jit(solution)/shard_map/ppermute | solution.py:182
  85.0 12.3 %collective-permute-start.16 = (bf16[2,4,128,128]{3,2,1,0:T(8,128)(2,1)S(1)}, bf16[2,4,128,128]{3,2,1,0:T(8,128)(2,1)S(1)}, u32[]{:S(2)}, u32[]{:S(2)}) collective-permute-start(bf16[2,4,128,128]{3,2,1,0:T(8,128)(2,1)S(1)} %bitcast.318), channel_id=1, source_target_pairs={{0,16},{8,24},{16,0},{24,8},{1,17},{9,25},{17,1},{25,9},{2,18},{10... | collective-permute-start | bytes 786440 | tf_op jit(solution)/shard_map/ppermute | solution.py:182
  123.9 13.6 %collective-permute-start.29 = (f32[4,32,512]{2,1,0:T(8,128)S(1)}, f32[4,32,512]{2,1,0:T(8,128)S(1)}, u32[]{:S(2)}, u32[]{:S(2)}) collective-permute-start(f32[4,32,512]{2,1,0:T(8,128)S(1)} %get-tuple-element.105), channel_id=1, source_target_pairs={{0,16},{8,24},{16,0},{24,8},{1,17},{9,25},{17,1},{25,9},{2,18},{10... | collective-permute-start | bytes 786440 | tf_op jit(solution)/shard_map/ppermute | solution.py:182
  125.4 12.0 %collective-permute-start.28 = (f32[4,32,512]{2,1,0:T(8,128)S(1)}, f32[4,32,512]{2,1,0:T(8,128)S(1)}, u32[]{:S(2)}, u32[]{:S(2)}) collective-permute-start(f32[4,32,512]{2,1,0:T(8,128)S(1)} %get-tuple-element.105), channel_id=1, source_target_pairs={{0,8},{8,0},{16,24},{24,16},{1,9},{9,1},{17,25},{25,17},{2,10},{10... | collective-permute-start | bytes 786440 | tf_op jit(solution)/shard_map/ppermute | solution.py:182
  169.1 22.0 %collective-permute-start.33 = (bf16[2,512,128]{2,1,0:T(8,128)(2,1)S(1)}, bf16[2,512,128]{2,1,0:T(8,128)(2,1)S(1)}, u32[]{:S(2)}, u32[]{:S(2)}) collective-permute-start(bf16[2,512,128]{2,1,0:T(8,128)(2,1)S(1)} %convolution_convert_fusion.2), channel_id=1, source_target_pairs={{0,2},{1,3},{2,0},{3,1},{4,6},{5,7},{6,4},{7,5},{8,10},{9,11},{10,... | collective-permute-start | bytes 786440 | tf_op jit(solution)/shard_map/ppermute | solution.py:182
  169.1 22.0 %collective-permute-start.32 = (bf16[2,512,128]{2,1,0:T(8,128)(2,1)S(1)}, bf16[2,512,128]{2,1,0:T(8,128)(2,1)S(1)}, u32[]{:S(2)}, u32[]{:S(2)}) collective-permute-start(bf16[2,512,128]{2,1,0:T(8,128)(2,1)S(1)} %convolution_convert_fusion.2), channel_id=1, source_target_pairs={{0,1},{1,0},{2,3},{3,2},{4,5},{5,4},{6,7},{7,6},{8,9},{9,8},{10,11... | collective-permute-start | bytes 786440 | tf_op jit(solution)/shard_map/ppermute | solution.py:182
  196.1 15.3 %collective-permute-start.38 = (bf16[2,4,128,128]{3,2,1,0:T(8,128)(2,1)S(1)}, bf16[2,4,128,128]{3,2,1,0:T(8,128)(2,1)S(1)}, u32[]{:S(2)}, u32[]{:S(2)}) collective-permute-start(bf16[2,4,128,128]{3,2,1,0:T(8,128)(2,1)S(1)} %add_convert_fusion), channel_id=1, source_target_pairs={{0,24},{8,16},{16,8},{24,0},{1,25},{9,17},{17,9},{25,1},{2,26},{10... | collective-permute-start | bytes 786440 | tf_op jit(solution)/shard_map/ppermute | solution.py:182
  197.4 13.9 %collective-permute-start.37 = (bf16[2,4,128,128]{3,2,1,0:T(8,128)(2,1)S(1)}, bf16[2,4,128,128]{3,2,1,0:T(8,128)(2,1)S(1)}, u32[]{:S(2)}, u32[]{:S(2)}) collective-permute-start(bf16[2,4,128,128]{3,2,1,0:T(8,128)(2,1)S(1)} %add_convert_fusion), channel_id=1, source_target_pairs={{0,16},{8,24},{16,0},{24,8},{1,17},{9,25},{17,1},{25,9},{2,18},{10... | collective-permute-start | bytes 786440 | tf_op jit(solution)/shard_map/ppermute | solution.py:182
  198.9 12.7 %collective-permute-start.36 = (bf16[2,4,128,128]{3,2,1,0:T(8,128)(2,1)S(1)}, bf16[2,4,128,128]{3,2,1,0:T(8,128)(2,1)S(1)}, u32[]{:S(2)}, u32[]{:S(2)}) collective-permute-start(bf16[2,4,128,128]{3,2,1,0:T(8,128)(2,1)S(1)} %add_convert_fusion), channel_id=1, source_target_pairs={{0,8},{8,0},{16,24},{24,16},{1,9},{9,1},{17,25},{25,17},{2,10},{10... | collective-permute-start | bytes 786440 | tf_op jit(solution)/shard_map/ppermute | solution.py:182
  236.7 13.5 %collective-permute-start.47 = (f32[4,32,512]{2,1,0:T(8,128)S(1)}, f32[4,32,512]{2,1,0:T(8,128)S(1)}, u32[]{:S(2)}, u32[]{:S(2)}) collective-permute-start(f32[4,32,512]{2,1,0:T(8,128)S(1)} %get-tuple-element.74), channel_id=1, source_target_pairs={{0,16},{8,24},{16,0},{24,8},{1,17},{9,25},{17,1},{25,9},{2,18},{10... | collective-permute-start | bytes 786440 | tf_op jit(solution)/shard_map/ppermute | solution.py:182
  238.1 12.0 %collective-permute-start.46 = (f32[4,32,512]{2,1,0:T(8,128)S(1)}, f32[4,32,512]{2,1,0:T(8,128)S(1)}, u32[]{:S(2)}, u32[]{:S(2)}) collective-permute-start(f32[4,32,512]{2,1,0:T(8,128)S(1)} %get-tuple-element.74), channel_id=1, source_target_pairs={{0,8},{8,0},{16,24},{24,16},{1,9},{9,1},{17,25},{25,17},{2,10},{10... | collective-permute-start | bytes 786440 | tf_op jit(solution)/shard_map/ppermute | solution.py:182
  (37 other events, 274.4 us)
Sparse Core Ops, SparseCore 0:
  240.9 30.8 reduce-scatter.3
